TPU v7x, 32 devices: a whole 2x2x4 slice. The times are simulated.
32 devices in a mesh: samp: 8 (over z, x), head: 4 (over y, core).
Axes of the slice: x: 2, y: 2, z: 4, core: 2. Of those that a mesh axis runs over, the one named last changes fastest.
Arguments:
- single: bfloat16 [64, 768, 768], P('samp', 'head'), may hold values from -6 to 6
- cond: bfloat16 [64, 768, 384], P('samp', 'head'), may hold values from -6 to 6
- pair: bfloat16 [2, 768, 768, 128], P(None, 'head', 'samp'), may hold values from -6 to 6
- complex_length: int32 [2], replicated, may hold values from 384 to 768, as said below
- sample_complex: int32 [64], P('samp'), may hold values from 0 to 1
- cotangent: bfloat16 [64, 768, 768], P('samp', 'head'), may hold values from -6 to 6
- gain_one: bfloat16 [384], replicated, may hold values from 0.5 to 1.5
- w_scale_one: bfloat16 [384, 768], replicated, may hold values from -0.3125 to 0.3125
- b_scale_one: bfloat16 [768], replicated, may hold values from -3 to 3
- w_shift_one: bfloat16 [384, 768], replicated, may hold values from -0.3125 to 0.3125
- w_query: bfloat16 [768, 768], replicated, may hold values from -0.21875 to 0.21875
- b_query: bfloat16 [768], replicated, may hold values from -3 to 3
- w_key: bfloat16 [768, 768], replicated, may hold values from -0.21875 to 0.21875
- w_value: bfloat16 [768, 768], replicated, may hold values from -0.21875 to 0.21875
- w_gate: bfloat16 [768, 768], replicated, may hold values from -0.21875 to 0.21875
- w_out: bfloat16 [768, 768], replicated, may hold values from -0.875 to 0.875
- w_pair: bfloat16 [128, 16], replicated, may hold values from -0.5 to 0.5
- w_attn_cond: bfloat16 [384, 768], replicated, may hold values from -0.3125 to 0.3125
- b_attn_cond: bfloat16 [768], replicated, may hold values from -3 to 3
- gain_two: bfloat16 [384], replicated, may hold values from 0.5 to 1.5
- w_scale_two: bfloat16 [384, 768], replicated, may hold values from -0.3125 to 0.3125
- b_scale_two: bfloat16 [768], replicated, may hold values from -3 to 3
- w_shift_two: bfloat16 [384, 768], replicated, may hold values from -0.3125 to 0.3125
- w_hidden_gate: bfloat16 [768, 1536], replicated, may hold values from -0.21875 to 0.21875
- w_hidden_up: bfloat16 [768, 1536], replicated, may hold values from -0.21875 to 0.21875
- w_hidden_down: bfloat16 [1536, 768], replicated, may hold values from -0.15625 to 0.15625
- w_tr_cond: bfloat16 [384, 768], replicated, may hold values from -0.3125 to 0.3125
- b_tr_cond: bfloat16 [768], replicated, may hold values from -3 to 3
Outputs:
- block_out: bfloat16 [64, 768, 768], P('samp', 'head')
- grad_single: float32 [64, 768, 768], P('samp', 'head')
- grad_pair: float32 [2, 768, 768, 128], P(None, 'head', 'samp')
- grad_gain_one: float32 [384], replicated
- grad_w_scale_one: float32 [384, 768], P('samp', 'head')
- grad_b_scale_one: float32 [768], replicated
- grad_w_shift_one: float32 [384, 768], P('samp', 'head')
- grad_w_query: float32 [768, 768], P('samp', 'head')
- grad_b_query: float32 [768], replicated
- grad_w_key: float32 [768, 768], P('samp', 'head')
- grad_w_value: float32 [768, 768], P('samp', 'head')
- grad_w_gate: float32 [768, 768], P('samp', 'head')
- grad_w_out: float32 [768, 768], P('samp', 'head')
- grad_w_pair: float32 [128, 16], replicated
- grad_w_attn_cond: float32 [384, 768], P('samp', 'head')
- grad_b_attn_cond: float32 [768], replicated
- grad_gain_two: float32 [384], replicated
- grad_w_scale_two: float32 [384, 768], P('samp', 'head')
- grad_b_scale_two: float32 [768], replicated
- grad_w_shift_two: float32 [384, 768], P('samp', 'head')
- grad_w_hidden_gate: float32 [768, 1536], P('samp', 'head')
- grad_w_hidden_up: float32 [768, 1536], P('samp', 'head')
- grad_w_hidden_down: float32 [1536, 768], P('samp', 'head')
- grad_w_tr_cond: float32 [384, 768], P('samp', 'head')
- grad_b_tr_cond: float32 [768], replicated
Inputs may be any that keep to these rules, and one draw needn't show every extreme that they name: A sample attends to the first complex_length tokens of its complex; one complex, drawn from the seed, has more than 672.
All inputs are finite; a program needn't handle non-finite values.
Results may differ from a plain program's by a relative error of at most 0.017.
Values may be sent and summed in bfloat16 or wider, within the bound.
No kernel may reach another device: no remote copies, remote signals or barrier semaphores. Data moves between devices by JAX's collectives and lax.ppermute only.
A program may use at most 320 MiB of HBM per device.

v0:
```python
import functools
import math

import jax
import jax.numpy as jnp
from jax import lax
from jax.experimental import pallas as pl
from jax.experimental.pallas import tpu as pltpu
from jax.sharding import PartitionSpec as P

f32, bf16 = jnp.float32, jnp.bfloat16
epsilon = 1e-05
fill_value = -1e30
LOG2E = math.log2(math.e)
VMEM_BYTES = 60 << 20
PAIR_LINES = (8, 16, 24, 32, 64)
NN, NT, TN = ((1,), (0,)), ((1,), (1,)), ((0,), (0,))


LIGHT = pl.CostEstimate(flops=1 << 20, bytes_accessed=1 << 20, transcendentals=0)


def dot(a, b, dims):
    return lax.dot_general(a, b, (dims, ((), ())), preferred_element_type=f32)


def norm_rows(inputs):
    mean_val = jnp.mean(inputs, axis=-1, keepdims=True)
    centered = inputs - mean_val
    variance = jnp.mean(centered * centered, axis=-1, keepdims=True)
    inverse = lax.rsqrt(variance + epsilon)
    return (centered * inverse, inverse)


def norm_back(normed, inverse, upstream):
    mean_grad = jnp.mean(upstream, axis=-1, keepdims=True)
    mean_dot = jnp.mean(upstream * normed, axis=-1, keepdims=True)
    return inverse * (upstream - mean_grad - normed * mean_dot)


def tile_of(tokens, sizes=(8, 16, 32, 64, 128, 256)):
    return max(t for t in sizes if tokens % t == 0)


def fixed(shape):
    return pl.BlockSpec(shape, lambda *_: (0,) * len(shape), pipeline_mode=pl.Buffered(1))


META = 6


def attend_kernel(meta, x0, x1, x2, x3, w_ref, bq_ref, *rest, which, nh, hd, rows, jc, nchunk, qscale):
    bias_hbm = rest[:nchunk]
    o_ref, far_ref, p_ref, q_ref, k_ref, v_ref, l_ref, xs, ks, ss, bias_ref, sems = rest[nchunk:]
    b = pl.program_id(0)
    g = meta[0]
    cplx = meta[META + b]
    per_block = nchunk // 4

    def copies():
        return [
            pltpu.make_async_copy(
                bias_hbm[i] if which[i] is None else bias_hbm[i].at[which[i]],
                bias_ref.at[meta[META + pl.num_programs(0) + i]],
                sems.at[i],
            )
            for i in range(nchunk)
        ]

    @pl.when(b == 0)
    def _():
        for copy in copies():
            copy.start()

    for r, x in enumerate((x0, x1, x2, x3)):
        xs[r * rows : (r + 1) * rows, :] = x[0]
    wch = nh * hd
    q = dot(w_ref[0:wch, :], xs[0 : 2 * rows, :], NT) + bq_ref[...]
    q_ref[0] = (q * qscale).astype(bf16)
    kv = dot(w_ref[wch : 3 * wch, :], xs[...], NT).astype(bf16)
    k_ref[0] = kv[0:wch]
    v_ref[0] = kv[wch:]

    @pl.when(b == 0)
    def _():
        for copy in copies():
            copy.wait()

    ones = jnp.ones((16, kv.shape[1]), bf16)
    outs = []
    sums = []
    before = None
    for h in range(nh + 1):
        if h < nh:
            ks[h % 2, :, :] = jnp.transpose(k_ref[0, h * hd : (h + 1) * hd, :])
            qT = q_ref[0, h * hd : (h + 1) * hd, :]
        m = None
        for t in range(nchunk):
            part = slice(t * jc, (t + 1) * jc)
            if h < nh:
                s_idx = ((t // per_block) ^ g) * per_block + t % per_block
                s = dot(ks[h % 2, part, :], qT, NN) + bias_ref[s_idx, cplx, h].astype(f32)
                ss[h % 2, part, :] = s
                mt = jnp.max(s.reshape(jc // 8, 8, s.shape[1]), axis=0)
                m = mt if m is None else jnp.maximum(m, mt)
            if h > 0:
                p_ref[0, h - 1, part, :] = jnp.exp2(ss[(h - 1) % 2, part, :] - before).astype(bf16)
        if h < nh:
            m = jnp.max(m, axis=0, keepdims=True)
        if h > 0:
            va = jnp.concatenate([v_ref[0, (h - 1) * hd : h * hd, :], ones], axis=0)
            oT = dot(va, p_ref[0, h - 1], NN)
            l = oT[hd : hd + 1, :]
            outs.append(oT[:hd] / l)
            sums.append(l)
        before = m
    l_ref[0] = jnp.concatenate(sums, axis=0)
    o = jnp.transpose(jnp.concatenate(outs, axis=0)).astype(bf16)
    o_ref[0] = o[:rows]
    far_ref[0] = o[rows:]


def attend(meta, xb, wT, bq, biases, *, nh, hd):
    B, rows, C = xb[0].shape
    nchunk = len(biases)
    biases, which = zip(*biases)
    ncx, _, jc, qi = biases[0].shape[-4:]
    L = nchunk * jc
    wch = nh * hd
    kern = functools.partial(
        attend_kernel, which=which, nh=nh, hd=hd, rows=rows, jc=jc, nchunk=nchunk, qscale=LOG2E / math.sqrt(hd)
    )
    xspec = pl.BlockSpec((1, rows, C), lambda b, m: (b, 0, 0))
    per = lambda shape: pl.BlockSpec((1,) + shape, lambda b, m: (b,) + (0,) * len(shape))
    return pl.pallas_call(
        kern,
        grid_spec=pltpu.PrefetchScalarGridSpec(
            num_scalar_prefetch=1,
            grid=(B,),
            in_specs=[xspec] * 4
            + [fixed(wT.shape), fixed(bq.shape)]
            + [pl.BlockSpec(memory_space=pl.ANY)] * nchunk,
            out_specs=[
                per((rows, wch)),
                per((rows, wch)),
                per((nh, L, qi)),
                per((wch, qi)),
                per((wch, L)),
                per((wch, L)),
                per((nh, qi)),
            ],
            scratch_shapes=[
                pltpu.VMEM((L, C), bf16),
                pltpu.VMEM((2, L, hd), bf16),
                pltpu.VMEM((2, L, qi), f32),
                pltpu.VMEM((nchunk, ncx, nh, jc, qi), bf16),
                pltpu.SemaphoreType.DMA((nchunk,)),
            ],
        ),
        out_shape=[
            jax.ShapeDtypeStruct((B, rows, wch), bf16),
            jax.ShapeDtypeStruct((B, rows, wch), bf16),
            jax.ShapeDtypeStruct((B, nh, L, qi), bf16),
            jax.ShapeDtypeStruct((B, wch, qi), bf16),
            jax.ShapeDtypeStruct((B, wch, L), bf16),
            jax.ShapeDtypeStruct((B, wch, L), bf16),
            jax.ShapeDtypeStruct((B, nh, qi), f32),
        ],
        compiler_params=pltpu.CompilerParams(vmem_limit_bytes=VMEM_BYTES),
        cost_estimate=LIGHT,
        name="attend",
    )(meta, *xb, wT, bq, *biases)


def attend_back_kernel(
    meta, p_ref, q_ref, k_ref, v_ref, l_ref, o0, o1, do0, do1, *rest, base, nh, hd, jc, nchunk, scale, fast
):
    dq_ref, dkv_ref = rest[:2]
    vs, ds, acc = rest[-3:]
    b = pl.program_id(0)
    g = meta[0]
    cplx = meta[META + b]
    per_block = nchunk // 4
    wch = nh * hd
    L = nchunk * jc

    @pl.when(b == 0)
    def _():
        acc[...] = jnp.zeros_like(acc)

    dO = jnp.transpose(jnp.concatenate([do0[0], do1[0]], axis=0).astype(f32))
    O = jnp.transpose(jnp.concatenate([o0[0], o1[0]], axis=0).astype(f32))
    prod = dO * O
    qi = dO.shape[1]
    row = lax.broadcasted_iota(jnp.int32, (16, qi), 0)
    ones = jnp.ones((16, L), bf16)
    for h in range(nh + 1):
        if h < nh:
            hs = slice(h * hd, (h + 1) * hd)
            his = slice((base + h) * hd, (base + h + 1) * hd)
            linv = 1.0 / l_ref[0, base + h : base + h + 1, :]
            dOh = (dO[his] * linv).astype(bf16)
            delta = jnp.sum(prod[his], axis=0, keepdims=True) * linv
            hi = delta.astype(bf16).astype(f32)
            extra = jnp.where(row == 0, -hi, jnp.where(row == 1, hi - delta, 0.0)).astype(bf16)
            dOa = jnp.concatenate([dOh, extra], axis=0)
            vs[h % 2] = jnp.transpose(jnp.concatenate([v_ref[0, hs, :], ones], axis=0))
        if h > 0:
            ps = slice((h - 1) * hd, h * hd)
            dk_parts, dv_parts = [], []
            kk, qq = k_ref[0, ps, :], q_ref[0, ps, :]
        for t in range(nchunk):
            r, u = t // per_block, t % per_block
            s_idx = (r ^ g) * per_block + u
            ts = slice(t * jc, (t + 1) * jc)
            if h < nh:
                d = dot(vs[h % 2, ts, :], dOa, NN) * p_ref[0, h, ts, :].astype(f32)
                acc[s_idx, cplx, h] += d
                ds[h % 2, ts, :] = d.astype(bf16)
            if h > 0:
                dk_parts.append(dot(ds[(h - 1) % 2, ts, :], qq, NT))
                dv_parts.append(dot(p_ref[0, h - 1, ts, :], dO_before, NT))
        if h > 0:
            dq_ref[0, ps, :] = (dot(kk, ds[(h - 1) % 2], NN) * scale).astype(bf16)
            dk = jnp.transpose(jnp.concatenate(dk_parts, axis=0)) * (1.0 / LOG2E)
            dkv_ref[0, ps, :] = dk.astype(bf16)
            dv = jnp.transpose(jnp.concatenate(dv_parts, axis=0))
            dkv_ref[0, wch + (h - 1) * hd : wch + h * hd, :] = dv.astype(bf16)
        if h < nh:
            dO_before = dOh

    @pl.when(b == pl.num_programs(0) - 1)
    def _():
        if fast:
            for i in range(4):
                for e in range(2):
                    block = acc[meta[2 + i] * 2 + (meta[1] ^ e)].astype(bf16)
                    for c in range(block.shape[0]):
                        rest[2 + 2 * c + e][i] = block[c]
        else:
            rest[2][...] = acc[...].astype(bf16)


def attend_back(meta, p, q, k, v, l, o0, o1, do0, do1, nchunk, ncx, *, base, nh, hd, fast):
    B, held, L, qi = p.shape
    rows = o0.shape[1]
    jc = L // nchunk
    wch = nh * hd
    kern = functools.partial(
        attend_back_kernel, base=base, nh=nh, hd=hd, jc=jc, nchunk=nchunk, scale=1.0 / math.sqrt(hd), fast=fast
    )
    per = lambda shape: pl.BlockSpec((1,) + shape, lambda b, m: (b,) + (0,) * len(shape))
    some = lambda shape: pl.BlockSpec((1,) + shape, lambda b, m: (b, base // nh) + (0,) * (len(shape) - 1))
    db = (nchunk, ncx, nh, jc, qi)
    outs = [((4,) + db[2:], bf16)] * (2 * ncx) if fast else [(db, bf16)]
    return pl.pallas_call(
        kern,
        grid_spec=pltpu.PrefetchScalarGridSpec(
            num_scalar_prefetch=1,
            grid=(B,),
            in_specs=[some((nh, L, qi)), some((wch, qi)), some((wch, L)), some((wch, L)), per((held, qi))]
            + [per((rows, held * hd))] * 4,
            out_specs=[per((wch, qi)), per((2 * wch, L))] + [fixed(s) for s, _ in outs],
            scratch_shapes=[
                pltpu.VMEM((2, L, hd + 16), bf16),
                pltpu.VMEM((2, L, qi), bf16),
                pltpu.VMEM(db, f32),
            ],
        ),
        out_shape=[jax.ShapeDtypeStruct((B, wch, qi), bf16), jax.ShapeDtypeStruct((B, 2 * wch, L), bf16)]
        + [jax.ShapeDtypeStruct(s, d) for s, d in outs],
        compiler_params=pltpu.CompilerParams(vmem_limit_bytes=VMEM_BYTES),
        cost_estimate=LIGHT,
        name="attend_back",
    )(meta, p, q, k, v, l, o0, o1, do0, do1)


def heads_back_kernel(meta, x0, x1, x2, x3, wq_ref, wkv_ref, *rest, parts, rows, wch, fast, chained):
    n = len(parts)
    dqs, dkvs, rest = rest[:n], rest[n : 2 * n], rest[2 * n :]
    if chained:
        start_b, start_q, start_kv = rest[:3]
        rest = rest[3:]
    near_ref, cross_ref, far_ref, own_ref, gb_ref = rest[:5]
    if fast:
        keep_ref, send_ref, xs, dq, dkv, gq, gkv, gt = rest[5:]
    else:
        gq, gkv, xs, dq, dkv = rest[5:]
    b = pl.program_id(0)

    @pl.when(b == 0)
    def _():
        gq[...] = start_q[...] if chained else jnp.zeros_like(gq)
        gkv[...] = start_kv[...] if chained else jnp.zeros_like(gkv)
        gb_ref[...] = start_b[...] if chained else jnp.zeros_like(gb_ref)

    for r, x in enumerate((x0, x1, x2, x3)):
        xs[r * rows : (r + 1) * rows, :] = x[0]
    for (chunk, at, size), q, kv in zip(parts, dqs, dkvs):
        start = chunk * wch + at
        dq[start : start + size, :] = q[0]
        start = 2 * chunk * wch + at
        dkv[start : start + size, :] = kv[0, :size]
        dkv[start + wch : start + wch + size, :] = kv[0, size:]
    q, kv = dq[...], dkv[...]
    gb_ref[...] += jnp.sum(q.astype(f32), axis=1, keepdims=True)
    gq[...] += dot(q, xs[0 : 2 * rows, :], NN)
    gkv[...] += dot(kv, xs[...], NN)
    kv = jnp.transpose(kv)
    q = jnp.transpose(q)
    dx = dot(kv[2 * rows :], wkv_ref[...], NN).astype(bf16)
    far_ref[0] = dx[:rows]
    cross_ref[0] = dx[rows:]
    dx = (dot(kv[: 2 * rows], wkv_ref[...], NN) + dot(q, wq_ref[...], NN)).astype(bf16)
    own_ref[0] = dx[:rows]
    near_ref[0] = dx[rows:]

    if fast:

        @pl.when(b == pl.num_programs(0) - 1)
        def _():
            for e, ref in enumerate((keep_ref, send_ref)):
                chunk = (meta[0] // 2) ^ e
                half = pl.ds(pl.multiple_of(chunk * wch, wch), wch)
                gt[:, 0:wch] = jnp.transpose(gq[half, :])
                both = pl.ds(pl.multiple_of(chunk * 2 * wch, wch), 2 * wch)
                gt[:, wch:] = jnp.transpose(gkv[both, :])
                count = gt.shape[0] // 8
                for i in range(8):
                    ref[i] = gt[emit_rows(meta, i, count), :].astype(bf16)


def heads_back(meta, xb, wq, wkv, grads, parts, *, wch, fast, span=None, start=()):
    rows, C = xb[0].shape[1:]
    off, B = span or (0, xb[0].shape[0])
    L = 4 * rows
    total = wq.shape[0]
    row = pl.BlockSpec((1, rows, C), lambda b, m: (b, 0, 0))
    row_in = pl.BlockSpec((1, rows, C), lambda b, m: (b + off, 0, 0))
    per = lambda shape: pl.BlockSpec((1,) + shape, lambda b, m: (b + off,) + (0,) * len(shape))
    dqs, dkvs = [g[0] for g in grads], [g[1] for g in grads]
    sums = [((total, C), f32), ((2 * total, C), f32)]
    held = [pltpu.VMEM((L, C), bf16), pltpu.VMEM((total, 2 * rows), bf16), pltpu.VMEM((2 * total, L), bf16)]
    if fast:
        outs = [((8, C // 8, 3 * wch), bf16)] * 2
        held += [pltpu.VMEM(s, d) for s, d in sums] + [pltpu.VMEM((C, 3 * wch), f32)]
    else:
        outs = sums
    outs = [((total, 1), f32)] + outs
    return pl.pallas_call(
        functools.partial(heads_back_kernel, parts=parts, rows=rows, wch=wch, fast=fast, chained=bool(start)),
        grid_spec=pltpu.PrefetchScalarGridSpec(
            num_scalar_prefetch=1,
            grid=(B,),
            in_specs=[row_in] * 4
            + [fixed(wq.shape), fixed(wkv.shape)]
            + [per(v.shape[1:]) for v in dqs + dkvs]
            + [fixed(v.shape) for v in start],
            out_specs=[row] * 4 + [fixed(s) for s, _ in outs],
            scratch_shapes=held,
        ),
        out_shape=[jax.ShapeDtypeStruct((B, rows, C), bf16)] * 4 + [jax.ShapeDtypeStruct(s, d) for s, d in outs],
        compiler_params=pltpu.CompilerParams(vmem_limit_bytes=VMEM_BYTES),
        cost_estimate=LIGHT,
        name="heads_back",
    )(meta, *xb, wq, wkv, *dqs, *dkvs, *start)


def blocked(w, count):
    across, heads = w.shape
    wide = jnp.tile(jnp.transpose(w), (count, count))
    row = lax.broadcasted_iota(jnp.int32, wide.shape, 0) // heads
    column = lax.broadcasted_iota(jnp.int32, wide.shape, 1) // across
    return jnp.where(row == column, wide, jnp.zeros_like(wide))


def pair_bias_kernel(meta, lens, pair_ref, wb_ref, low_ref, inv_ref, raw_ref, *rest, few, blocks, group):
    outs, scr = rest[:-1], rest[-1]
    c, t = pl.program_id(0), pl.program_id(1)
    lines, columns, cz = pair_ref.shape[1:]
    heads = few * blocks
    per = lines // group
    mean = jnp.full((cz, cz), 1.0 / cz, bf16)
    lane = lax.broadcasted_iota(jnp.int32, (columns, group * heads), 1) // heads
    table = []
    for n in range(per):
        x = [pair_ref[0, n * group + i] for i in range(group)]
        flat = columns % 16 == 0
        if flat:
            x = [jnp.concatenate(x, axis=0)]
        lows, inverses = [], []
        for v in x:
            centered = v.astype(f32) - dot(v, mean, NN)
            inverse = lax.rsqrt(dot((centered * centered).astype(bf16), mean, NN) + epsilon)
            lows.append((centered * inverse).astype(bf16))
            inverses.append(inverse)
        if flat:
            lows = [lows[0][i * columns : (i + 1) * columns] for i in range(group)]
            inverses = [inverses[0][i * columns : (i + 1) * columns] for i in range(group)]
        spread = inverses[0][:, : group * heads]
        for i in range(1, group):
            spread = jnp.where(lane == i, inverses[i][:, : group * heads], spread)
        inv_ref[0, n] = spread
        for i in range(group):
            low_ref[0, n * group + i] = lows[i]
        table.append(jnp.concatenate(lows, axis=1))
    out = dot(jnp.concatenate(table, axis=0), wb_ref[...], NT)
    for n in range(per):
        part = out[n * columns : (n + 1) * columns]
        raw_ref[0, n] = part
        start = pl.multiple_of((t * per + n) * group * heads, group * heads)
        scr[pl.ds(start, group * heads), :] = jnp.transpose(part)

    @pl.when(t == pl.num_programs(1) - 1)
    def _():
        core = meta[0] % 2
        rows = scr.shape[0] // heads
        place = lax.broadcasted_iota(jnp.int32, (columns, rows), 0) + meta[1] * columns
        valid = place < lens[c]
        half = len(outs) // 2
        for k in range(half):
            for f in range(few):
                for e in range(2):
                    h = (2 * k + (core ^ e)) * few + f
                    v = jnp.transpose(scr[pl.ds(h, rows, stride=heads), :])
                    outs[e * half + k][0, f] = jnp.where(valid, v * LOG2E, fill_value).astype(bf16)


def pair_specs(pair, heads, group):
    lines = tile_of(pair.shape[1], PAIR_LINES)
    columns, cz = pair.shape[2:]
    return (
        lines,
        pl.BlockSpec((1, lines, columns, cz), lambda c, t, *_: (c, t, 0, 0)),
        pl.BlockSpec((1, lines // group, columns, group * heads), lambda c, t, *_: (c, t, 0, 0)),
        jax.ShapeDtypeStruct((pair.shape[0], pair.shape[1] // group, columns, group * heads), f32),
    )


def pair_bias(meta, lens, pair, wb, *, few, blocks, group):
    ncx, rows, columns, cz = pair.shape
    heads = few * blocks
    lines, spec, thin, thin_shape = pair_specs(pair, heads, group)
    out = jax.ShapeDtypeStruct((ncx, few, columns, rows), bf16)
    return pl.pallas_call(
        functools.partial(pair_bias_kernel, few=few, blocks=blocks, group=group),
        grid_spec=pltpu.PrefetchScalarGridSpec(
            num_scalar_prefetch=2,
            grid=(ncx, rows // lines),
            in_specs=[spec, fixed(wb.shape)],
            out_specs=[spec, thin, thin]
            + [pl.BlockSpec((1, few, columns, rows), lambda c, t, *_: (c, 0, 0, 0))] * blocks,
            scratch_shapes=[pltpu.VMEM((rows * heads, columns), f32)],
        ),
        out_shape=[jax.ShapeDtypeStruct(pair.shape, bf16), thin_shape, thin_shape] + [out] * blocks,
        compiler_params=pltpu.CompilerParams(vmem_limit_bytes=VMEM_BYTES),
        cost_estimate=LIGHT,
        name="pair_bias",
    )(meta, lens, pair, wb)


def pair_back_kernel(meta, low_ref, inv_ref, raw_ref, w2_ref, mean_ref, *rest, few, blocks, group):
    grads = rest[:blocks]
    out_ref, gw_ref, scr, acc = rest[blocks:]
    c, t = pl.program_id(0), pl.program_id(1)
    lines, columns, cz = low_ref.shape[1:]
    heads = few * blocks
    per = lines // group

    @pl.when((c == 0) & (t == 0))
    def _():
        acc[...] = jnp.zeros_like(acc)

    @pl.when(t == 0)
    def _():
        core = meta[0] % 2
        rows = scr.shape[0] // heads
        half = blocks // 2
        for k in range(half):
            for f in range(few):
                for e in range(2):
                    h = (2 * k + (core ^ e)) * few + f
                    scr[pl.ds(h, rows, stride=heads), :] = jnp.transpose(grads[e * half + k][0, f].astype(f32))

    ds, prods, xs = [], [], []
    for n in range(per):
        start = pl.multiple_of((t * per + n) * group * heads, group * heads)
        x = jnp.transpose(scr[pl.ds(start, group * heads), :])
        d = x * inv_ref[0, n]
        prod = d * raw_ref[0, n]
        hi = prod.astype(bf16)
        d = d.astype(bf16)
        xs.append(x.astype(bf16))
        ds.append(jnp.concatenate([d, d], axis=1))
        prods.append(jnp.concatenate([hi, (prod - hi.astype(f32)).astype(bf16)], axis=1))
    upstream = dot(jnp.concatenate(ds, axis=0), w2_ref[...], NN)
    along = dot(jnp.concatenate(prods, axis=0), mean_ref[...], NN)
    table = []
    for n in range(per):
        lows = [low_ref[0, n * group + i] for i in range(group)]
        ns = slice(n * columns, (n + 1) * columns)
        for i in range(group):
            zs = slice(i * cz, (i + 1) * cz)
            out_ref[0, n * group + i] = upstream[ns, zs] - lows[i].astype(f32) * along[ns, zs]
        table.append(jnp.concatenate(lows, axis=1))
    acc[...] += dot(jnp.concatenate(xs, axis=0), jnp.concatenate(table, axis=0), TN)

    @pl.when((c == pl.num_programs(0) - 1) & (t == pl.num_programs(1) - 1))
    def _():
        total = acc[0:heads, 0:cz]
        for i in range(1, group):
            total += acc[i * heads : (i + 1) * heads, i * cz : (i + 1) * cz]
        gw_ref[...] = total


def pair_back(meta, low, inv, raw, w, grads, *, few, blocks, group):
    ncx, rows, columns, cz = low.shape
    heads = few * blocks
    lines, spec, thin, _ = pair_specs(low, heads, group)
    mean = jnp.mean(w.astype(f32), axis=0, keepdims=True)
    w2 = jnp.concatenate([blocked(w, group), blocked(jnp.broadcast_to(-mean, w.shape).astype(bf16), group)], axis=0)
    ones = blocked(jnp.full(w.shape, 1.0 / cz, bf16), group)
    ones = jnp.concatenate([ones, ones], axis=0)
    return pl.pallas_call(
        functools.partial(pair_back_kernel, few=few, blocks=blocks, group=group),
        grid_spec=pltpu.PrefetchScalarGridSpec(
            num_scalar_prefetch=1,
            grid=(ncx, rows // lines),
            in_specs=[spec, thin, thin, fixed(w2.shape), fixed(ones.shape)]
            + [pl.BlockSpec((1, few, columns, rows), lambda c, t, *_: (c, 0, 0, 0))] * blocks,
            out_specs=[spec, fixed((heads, cz))],
            scratch_shapes=[pltpu.VMEM((rows * heads, columns), f32), pltpu.VMEM((group * heads, group * cz), f32)],
        ),
        out_shape=[jax.ShapeDtypeStruct(low.shape, f32), jax.ShapeDtypeStruct((heads, cz), f32)],
        compiler_params=pltpu.CompilerParams(vmem_limit_bytes=VMEM_BYTES),
        cost_estimate=LIGHT,
        name="pair_back",
    )(meta, low, inv, raw, w2, ones, *grads)


def column_sum(v):
    return jnp.sum(v, axis=0, keepdims=True)


def tiled(rows, width, steps):
    return pl.BlockSpec((rows, width), lambda t, *_: (jnp.minimum(t, steps - 1), 0))


def adapt_kernel(single_ref, cond_ref, gain, w_scale, b_scale, w_shift, x_ref):
    normed, _ = norm_rows(single_ref[...].astype(f32))
    cond_hat, _ = norm_rows(cond_ref[...].astype(f32))
    cond_low = (cond_hat * gain[...].astype(f32)).astype(bf16)
    gate = jax.nn.sigmoid(dot(cond_low, w_scale[...], NN) + b_scale[...].astype(f32))
    x_ref[...] = (gate * normed + dot(cond_low, w_shift[...], NN)).astype(bf16)


def adapt(single, cond, gain, w_scale, b_scale, w_shift):
    tokens, width = single.shape
    tile = tile_of(tokens)
    steps = tokens // tile
    return pl.pallas_call(
        adapt_kernel,
        grid=(steps,),
        in_specs=[tiled(tile, width, steps), tiled(tile, cond.shape[1], steps)]
        + [fixed(v.shape) for v in (gain, w_scale, b_scale, w_shift)],
        out_specs=tiled(tile, width, steps),
        out_shape=jax.ShapeDtypeStruct((tokens, width), bf16),
        compiler_params=pltpu.CompilerParams(vmem_limit_bytes=VMEM_BYTES),
        cost_estimate=LIGHT,
        name="adapt",
    )(single, cond, gain, w_scale, b_scale, w_shift)


def emit_rows(meta, step, count):
    place = meta[2 + step % 4] * 2 + (meta[1] ^ (step // 4))
    return pl.ds(pl.multiple_of(place * count, count), count)


def before_kernel(
    x_ref, cond_ref, cot_ref, w_gate, w_ac, b_ac, gain, w_scale, b_scale, w_shift, w_dn, w_tc, b_tc,
    gate_ref, acond_ref, tcond_ref, scale_ref, shift_ref, dh_ref,
):
    cond = cond_ref[...]
    tcond = jax.nn.sigmoid(dot(cond, w_tc[...], NN) + b_tc[...].astype(f32))
    tcond_ref[...] = tcond.astype(tcond_ref.dtype)
    d_tr = (tcond * cot_ref[...].astype(f32)).astype(bf16)
    dh_ref[...] = dot(d_tr, w_dn[...], NT).astype(dh_ref.dtype)
    acond_ref[...] = jax.nn.sigmoid(dot(cond, w_ac[...], NN) + b_ac[...].astype(f32)).astype(acond_ref.dtype)
    cond_hat, _ = norm_rows(cond.astype(f32))
    cond_low = (cond_hat * gain[...].astype(f32)).astype(bf16)
    scale = jax.nn.sigmoid(dot(cond_low, w_scale[...], NN) + b_scale[...].astype(f32))
    scale_ref[...] = scale.astype(scale_ref.dtype)
    shift_ref[...] = dot(cond_low, w_shift[...], NN).astype(shift_ref.dtype)
    gate_ref[...] = jax.nn.sigmoid(dot(x_ref[...], w_gate[...], NN)).astype(gate_ref.dtype)


def before(x_one, cond, cot, weights):
    w_gate, w_out, w_ac, b_ac, gain, w_scale, b_scale, w_shift, w_hg, w_hu, w_dn, w_tc, b_tc = weights
    used = (w_gate, w_ac, b_ac, gain, w_scale, b_scale, w_shift, w_dn, w_tc, b_tc)
    tokens, width = x_one.shape
    tile = tile_of(tokens)
    steps = tokens // tile
    outs = [(width, f32)] * 4 + [(width, bf16), (w_dn.shape[0], bf16)]
    return pl.pallas_call(
        before_kernel,
        grid=(steps,),
        in_specs=[tiled(tile, w, steps) for w in (width, cond.shape[1], width)] + [fixed(w.shape) for w in used],
        out_specs=[tiled(tile, w, steps) for w, _ in outs],
        out_shape=[jax.ShapeDtypeStruct((tokens, w), d) for w, d in outs],
        compiler_params=pltpu.CompilerParams(vmem_limit_bytes=VMEM_BYTES),
        cost_estimate=LIGHT,
        name="before",
    )(x_one, cond, cot, *used)


def middle_kernel(
    meta, x_ref, single_ref, cond_ref, cot_ref, gate_ref, acond_ref, tcond_ref, scale_ref, shift_ref, dh_ref,
    a0, a1, a2, a3, w_gate, w_out, gain, w_scale, w_shift, w_hg, w_hu, w_dn,
    out_ref, dmid_ref, dxg_ref, da0, da1, da2, da3, s_ac, s_scale, s_tc, s_gain, *rest, tiles, fast,
):
    core = meta[0] % 2
    step = pl.program_id(0)
    if fast:
        out_w, g_hidden, g_square, g_cond, g_norm, g_dn = rest
    else:
        g_hidden, g_square, g_cond, g_norm, g_dn = rest

    @pl.when(step == 0)
    def _():
        for ref in (g_hidden, g_square, g_cond, g_norm, g_dn, s_ac, s_scale, s_tc, s_gain):
            ref[...] = jnp.zeros_like(ref)

    @pl.when(step < tiles)
    def _():
        cond = cond_ref[...]
        first = core == 0

        def attended():
            return jnp.concatenate(
                [
                    jnp.where(first, a0[...], a1[...]),
                    jnp.where(first, a1[...], a0[...]),
                    jnp.where(first, a2[...], a3[...]),
                    jnp.where(first, a3[...], a2[...]),
                ],
                axis=1,
            ).astype(f32)

        gated = (attended() * gate_ref[...]).astype(bf16)
        branch = dot(gated, w_out[...], NN)
        mid = single_ref[...].astype(f32) + acond_ref[...] * branch
        normed, inverse = norm_rows(mid)
        x_two = (scale_ref[...] * normed + shift_ref[...].astype(f32)).astype(bf16)
        hgate = dot(x_two, w_hg[...], NN)
        hup = dot(x_two, w_hu[...], NN)
        sig = jax.nn.sigmoid(hgate)
        silu = hgate * sig
        hidden = (silu * hup).astype(bf16)
        d_hidden = dh_ref[...].astype(f32)
        d_hg = (d_hidden * hup * sig * (1.0 + hgate * (1.0 - sig))).astype(bf16)
        d_hu = (d_hidden * silu).astype(bf16)
        tcond = tcond_ref[...]
        dy = cot_ref[...].astype(f32)
        tr_branch = dot(hidden, w_dn[...], NN)
        out_ref[...] = (mid + tcond * tr_branch).astype(bf16)
        d_trc = dy * tr_branch * tcond * (1.0 - tcond)
        s_tc[...] += column_sum(d_trc)
        g_cond[0] += dot(cond, d_trc.astype(bf16), TN)
        g_dn[...] += dot(hidden, (tcond * dy).astype(bf16), TN)
        g_hidden[0] += dot(x_two, d_hg, TN)
        g_hidden[1] += dot(x_two, d_hu, TN)
        g_two = dot(d_hg, w_hg[...], NT) + dot(d_hu, w_hu[...], NT)
        scale = scale_ref[...]
        cond_hat, _ = norm_rows(cond.astype(f32))
        cond_low = (cond_hat * gain[...].astype(f32)).astype(bf16)
        d_scale = g_two * normed * scale * (1.0 - scale)
        s_scale[...] += column_sum(d_scale)
        d_scale = d_scale.astype(bf16)
        d_shift = g_two.astype(bf16)
        g_norm[0] += dot(cond_low, d_scale, TN)
        g_norm[1] += dot(cond_low, d_shift, TN)
        d_cond = dot(d_scale, w_scale[...], NT) + dot(d_shift, w_shift[...], NT)
        s_gain[...] += column_sum(d_cond * cond_hat)
        d_mid = dy + norm_back(normed, inverse, g_two * scale)
        dmid_ref[...] = d_mid
        acond = acond_ref[...]
        d_attn = (acond * d_mid).astype(bf16)
        d_ac = d_mid * branch * acond * (1.0 - acond)
        s_ac[...] += column_sum(d_ac)
        g_cond[1] += dot(cond, d_ac.astype(bf16), TN)
        g_square[0] += dot(gated, d_attn, TN)
        d_gated = dot(d_attn, w_out[...], NT)
        gate = gate_ref[...]
        d_att = (d_gated * gate).astype(bf16)
        d_gate = (d_gated * attended() * gate * (1.0 - gate)).astype(bf16)
        g_square[1] += dot(x_ref[...], d_gate, TN)
        dxg_ref[...] = dot(d_gate, w_gate[...], NT).astype(bf16)
        q = d_att.shape[1] // 4
        parts = [d_att[:, i * q : (i + 1) * q] for i in range(4)]
        da0[...] = jnp.where(first, parts[0], parts[1])
        da1[...] = jnp.where(first, parts[1], parts[0])
        da2[...] = jnp.where(first, parts[2], parts[3])
        da3[...] = jnp.where(first, parts[3], parts[2])

    if fast:

        @pl.when(step >= tiles)
        def _():
            emit = step - tiles
            place = meta[2 + emit % 4] * 2 + (meta[1] ^ (emit // 4))
            for g in range(4):
                at = 0
                for one, two, count in (
                    (g_hidden.at[0], None, 8),
                    (g_hidden.at[1], None, 8),
                    (g_square.at[0], g_square.at[1], 8),
                    (g_cond.at[0], g_cond.at[1], 8),
                    (g_norm.at[0], g_norm.at[1], 8),
                    (g_dn, g_dn, 16),
                ):
                    n, lanes = one.shape[0] // count, one.shape[1] // 4
                    take = lambda ref, row: ref[pl.ds(pl.multiple_of(row, n), n), g * lanes : (g + 1) * lanes]
                    if two is None:
                        part = take(one, place * n)
                    elif one is two:
                        part = jnp.concatenate([take(one, 2 * place * n), take(one, (2 * place + 1) * n)], axis=1)
                    else:
                        part = jnp.concatenate([take(one, place * n), take(two, place * n)], axis=1)
                    out_w[g, 0, at : at + n, :] = part.astype(bf16)
                    at += n


def middle(meta, x_one, single, cond, cot, gates, atts, weights, fast):
    tokens, width = single.shape
    tile = tile_of(tokens)
    tiles = tokens // tile
    cs = cond.shape[1]
    quarter = atts[0].shape[1]
    w_gate, w_out, w_ac, b_ac, gain, w_scale, b_scale, w_shift, w_hg, w_hu, w_dn, w_tc, b_tc = weights
    fold = lambda n: jax.ShapeDtypeStruct((1, n), f32)
    sums = [fold(width), fold(width), fold(width), fold(cs)]
    grads = [(2,) + w_hg.shape, (2,) + w_out.shape, (2,) + w_ac.shape, (2,) + w_scale.shape, w_dn.shape]
    row_out = [(width, bf16), (width, f32), (width, bf16)] + [(quarter, bf16)] * 4
    used = (w_gate, w_out, gain, w_scale, w_shift, w_hg, w_hu, w_dn)
    if fast:
        lanes = width // 2
        rows = sum(w.size for w in weights if w.shape[0] > 1) // (8 * 4 * lanes)
        more_specs = [pl.BlockSpec((4, 1, rows, lanes), lambda t, *_: (0, jnp.maximum(t - tiles, 0), 0, 0))]
        more = [jax.ShapeDtypeStruct((4, 8, rows, lanes), bf16)]
        scratch = [pltpu.VMEM(g, f32) for g in grads]
    else:
        more_specs = [fixed(g) for g in grads]
        more = [jax.ShapeDtypeStruct(g, f32) for g in grads]
        scratch = []
    return pl.pallas_call(
        functools.partial(middle_kernel, tiles=tiles, fast=fast),
        grid_spec=pltpu.PrefetchScalarGridSpec(
            num_scalar_prefetch=1,
            grid=(tiles + 8 * fast,),
            in_specs=[tiled(tile, w, tiles) for w in (width, width, cs, width)]
            + [tiled(tile, v.shape[1], tiles) for v in gates]
            + [tiled(tile, quarter, tiles)] * 4
            + [fixed(w.shape) for w in used],
            out_specs=[tiled(tile, w, tiles) for w, _ in row_out] + [fixed(g.shape) for g in sums] + more_specs,
            scratch_shapes=scratch,
        ),
        out_shape=[jax.ShapeDtypeStruct((tokens, w), d) for w, d in row_out] + sums + more,
        compiler_params=pltpu.CompilerParams(vmem_limit_bytes=VMEM_BYTES),
        cost_estimate=LIGHT,
        name="middle",
    )(meta, x_one, single, cond, cot, *gates, *atts, *used)


def last_kernel(
    meta, d0, d1, d2, d3, d4, d5, d6, single_ref, cond_ref, dmid_ref, gain, w_scale, b_scale, w_shift,
    out_ref, s_scale, s_gain, *rest, fast,
):
    if fast:
        keep_ref, send_ref, g_norm = rest
    else:
        (g_norm,) = rest

    @pl.when(pl.program_id(0) == 0)
    def _():
        for ref in (g_norm, s_scale, s_gain):
            ref[...] = jnp.zeros_like(ref)

    late_half = pl.program_id(0) >= pl.num_programs(0) // 2
    g_one = d6[...].astype(f32)
    for one, two in ((d0, d1), (d2, d3), (d4, d5)):
        g_one += jnp.where(late_half, two[...], one[...]).astype(f32)
    normed, inverse = norm_rows(single_ref[...].astype(f32))
    cond_hat, _ = norm_rows(cond_ref[...].astype(f32))
    cond_low = (cond_hat * gain[...].astype(f32)).astype(bf16)
    scale = jax.nn.sigmoid(dot(cond_low, w_scale[...], NN) + b_scale[...].astype(f32))
    d_scale = g_one * normed * scale * (1.0 - scale)
    s_scale[...] += column_sum(d_scale)
    d_scale = d_scale.astype(bf16)
    d_shift = g_one.astype(bf16)
    g_norm[0] += dot(cond_low, d_scale, TN)
    g_norm[1] += dot(cond_low, d_shift, TN)
    d_cond = dot(d_scale, w_scale[...], NT) + dot(d_shift, w_shift[...], NT)
    s_gain[...] += column_sum(d_cond * cond_hat)
    out_ref[...] = dmid_ref[...] + norm_back(normed, inverse, g_one * scale)

    if fast:

        @pl.when(pl.program_id(0) == pl.num_programs(0) - 1)
        def _():
            n, wide = g_norm.shape[1] // 8, g_norm.shape[2] // 2
            for e, ref in enumerate((keep_ref, send_ref)):
                for p in range(2):
                    lanes = pl.ds(pl.multiple_of(((meta[0] // 2) ^ p) * wide, wide), wide)
                    for i in range(8):
                        ref[p, i] = g_norm[(meta[0] % 2) ^ e, emit_rows(meta, i, n), lanes].astype(bf16)


def last(meta, ds, single, cond, dmid, gain, w_scale, b_scale, w_shift, fast):
    tokens, width = single.shape
    tile = tile_of(tokens)
    steps = tokens // tile
    cs = cond.shape[1]
    grads = (2,) + w_scale.shape
    if fast:
        more = [jax.ShapeDtypeStruct((2, 8, cs // 8, width // 2), bf16)] * 2
        scratch = [pltpu.VMEM(grads, f32)]
    else:
        more = [jax.ShapeDtypeStruct(grads, f32)]
        scratch = []
    more = [jax.ShapeDtypeStruct((1, width), f32), jax.ShapeDtypeStruct((1, cs), f32)] + more
    row = tiled(tile, width, steps)
    half = steps // 2
    early_row = pl.BlockSpec((tile, width), lambda t, *_: (jnp.minimum(t, half - 1), 0))
    late_row = pl.BlockSpec((tile, width), lambda t, *_: (jnp.maximum(t - half, 0), 0))
    return pl.pallas_call(
        functools.partial(last_kernel, fast=fast),
        grid_spec=pltpu.PrefetchScalarGridSpec(
            num_scalar_prefetch=1,
            grid=(steps,),
            in_specs=[early_row, late_row] * 3
            + [row, row]
            + [tiled(tile, cs, steps), row]
            + [fixed(w.shape) for w in (gain, w_scale, b_scale, w_shift)],
            out_specs=[row] + [fixed(g.shape) for g in more],
            scratch_shapes=scratch,
        ),
        out_shape=[jax.ShapeDtypeStruct((tokens, width), f32)] + more,
        compiler_params=pltpu.CompilerParams(vmem_limit_bytes=VMEM_BYTES),
        cost_estimate=LIGHT,
        name="last",
    )(meta, *ds, single, cond, dmid, gain, w_scale, b_scale, w_shift)


def swap(value, bit):
    return lax.ppermute(value, "head", [(i, i ^ bit) for i in range(lax.axis_size("head"))])


def across(value):
    return lax.ppermute(value, "samp", [(i, i ^ 1) for i in range(8)])


def slot(value, bit):
    return lax.ppermute(value, "samp", [(i, i ^ (2 * bit)) for i in range(8)])


def add(*terms):
    total = terms[0].astype(f32)
    for term in terms[1:]:
        total = total + term.astype(f32)
    return total


def tie(value, *others):
    return lax.optimization_barrier((value,) + others)[0]


def low(*terms):
    return add(*terms).astype(bf16)


Z_ORDER = (0, 2, 1, 3)


def x_step(block):
    return block[:4], across(block[4:])


def z_first(keep, got):
    return slot(low(keep[2:], got[2:]), 1)


def z_second(keep, got, z_got):
    return slot(low(keep[1], got[1], z_got[1]), 2)


def z_total(keep, got, z_got, last_got):
    return add(keep[0], got[0], z_got[0], last_got)


def fence(*values):
    return lax.optimization_barrier(values)


def total_step(vector, step):
    if step < 2:
        return vector + swap(vector, 1 << step)
    if step == 2:
        return vector + across(vector)
    return vector + slot(vector, step - 2)


def pack_w(w_heads, wide):
    return (
        jnp.concatenate([w[:wide] for w in w_heads], axis=0),
        jnp.concatenate([w[wide:] for w in w_heads], axis=0),
    )


def on_device(
    single,
    cond,
    pair,
    complex_length,
    sample_complex,
    cotangent,
    gain_one,
    w_scale_one,
    b_scale_one,
    w_shift_one,
    w_query,
    b_query,
    w_key,
    w_value,
    w_gate,
    w_out,
    w_pair,
    w_attn_cond,
    b_attn_cond,
    gain_two,
    w_scale_two,
    b_scale_two,
    w_shift_two,
    w_hidden_gate,
    w_hidden_up,
    w_hidden_down,
    w_tr_cond,
    b_tr_cond,
):
    groups = lax.axis_size("head")
    devices = lax.axis_size("samp")
    me = lax.axis_index("head")
    place = lax.axis_index("samp")
    core = me % 2
    part = me // 2
    samples, rows, width = single.shape
    cs = cond.shape[2]
    tokens = samples * rows
    length = rows * groups
    heads = w_pair.shape[1]
    few = heads // groups
    dim = width // heads
    wide = few * dim
    complexes, _, columns, _ = pair.shape
    chunks = 2 * groups
    chunk = length // chunks
    halves = range(groups // 2)
    fast = devices == 8 and groups == 4 and columns == chunk
    line = lambda v: v.reshape(1, -1)
    flat = lambda v: v.reshape(tokens, width)
    first = core == 0

    if fast:
        z, x = place // 2, place % 2
        order = z ^ jnp.array(Z_ORDER, jnp.int32)
        slots = jnp.stack([order * 2 + x, order * 2 + 1 - x], axis=1).reshape(8)
    else:
        x = jnp.zeros((), jnp.int32)
        order, slots = jnp.zeros((4,), jnp.int32), jnp.arange(chunks, dtype=jnp.int32)
    meta = jnp.concatenate([jnp.stack([me, x]).astype(jnp.int32), order, sample_complex, slots])
    pair_meta = jnp.stack([me, place]).astype(jnp.int32)
    group = 8
    sizes = dict(few=few, blocks=groups, group=group)
    single_t, cond_t, cot_t = flat(single), cond.reshape(tokens, cs), flat(cotangent)
    weights_one = (line(gain_one), w_scale_one, line(b_scale_one), w_shift_one)
    weights_two = (
        w_gate, w_out, w_attn_cond, line(b_attn_cond), line(gain_two), w_scale_two, line(b_scale_two), w_shift_two,
        w_hidden_gate, w_hidden_up, w_hidden_down, w_tr_cond, line(b_tr_cond),
    )

    def own_heads(*weights):
        columns_of = lambda w, k: lax.dynamic_slice_in_dim(w, (2 * k + core) * wide, wide, w.ndim - 1)
        w_heads = [jnp.concatenate([columns_of(w, k).T for w in weights[:3]], axis=0) for k in halves]
        b_heads = [columns_of(weights[3].astype(f32), k)[:, None] for k in halves]
        return w_heads, b_heads, *pack_w(w_heads, wide)

    parts = [(k, 0, wide) for k in halves]
    by_sample = lambda v: v.reshape(samples, rows, -1)
    by_token = lambda v: v.reshape(-1, v.shape[-1])
    attend_one = lambda k, blocks, biases: attend(meta, blocks, w_heads[k], b_heads[k], biases, nh=few, hd=dim)
    middle_one = lambda x_one, gates, atts: middle(meta, x_one, single_t, cond_t, cot_t, gates, atts, weights_two, fast)
    back_one = lambda kept, own, near: attend_back(
        meta, *kept[2:], *kept[:2], own, near, chunks, complexes, base=0, nh=few, hd=dim, fast=fast
    )

    def q_sums(gb):
        zero = jnp.zeros((wide,), f32)
        out = []
        for k in halves:
            mine = gb[k * wide : (k + 1) * wide].reshape(-1)
            out += [jnp.where(first, mine, zero), jnp.where(first, zero, mine)]
        return out

    w_blocked = blocked(w_pair, group)
    pair_low, pair_inverse, pair_raw, *bias = pair_bias(pair_meta, complex_length, pair, w_blocked, **sizes)
    near_bias = [swap(v, 1) for v in bias[groups // 2 :]]
    owns = [jnp.concatenate([bias[k], near_bias[k]], axis=-1) for k in halves]

    if fast:
        both_owns = jnp.stack(owns)
        owns, both_owns, single_t = fence(owns, both_owns, single_t)
        far_0, z_0, x_own = slot(owns[0], 2), [slot(owns[0], 1)], across(both_owns)
        x_one = adapt(single_t, cond_t, *weights_one)
        far_0, z_0, x_own, x_one, owns = fence(far_0, z_0, x_own, x_one, owns)
        x_far = swap(x_one, 2)
        far_1 = slot(owns[1], 2)
        z_0.append(slot(far_0, 1))
        x_0 = [across(far_0), across(z_0[0])]
        far_1, z_0, x_0, owns, x_mid, qkv = fence(far_1, z_0, x_0, owns, x_one, (w_query, w_key, w_value, b_query))
        w_heads, b_heads, w_q, w_kv = own_heads(*qkv)
        x_0.append(across(z_0[1]))
        x_1 = [across(far_1)]
        z_1 = [slot(owns[1], 1), slot(far_1, 1)]
        gates = before(x_mid, cond_t, cot_t, weights_two)
        x_far, x_0, x_1, z_1, gates, x_mid, w_heads, b_heads, w_q, w_kv = fence(
            x_far, x_0, x_1, z_1, gates, x_mid, w_heads, b_heads, w_q, w_kv
        )
        x_cross, x_near = swap(x_far, 1), swap(x_mid, 1)
        x_1 += [across(v) for v in z_1]
        blocks = [by_sample(v) for v in (x_one, x_near, x_far, x_cross)]
        pairs_of = lambda k, here, there: [
            pair_of for v, w in zip(here, [(x_own, k)] + [(u, None) for u in there]) for pair_of in ((v, None), w)
        ]
        kept = [attend_one(0, blocks, pairs_of(0, [owns[0], far_0] + z_0, x_0))]
        kept, x_1 = fence(kept, x_1)
        near_atts = [swap(kept[0][1], 1)]
        kept.append(attend_one(1, blocks, pairs_of(1, [owns[1], far_1] + z_1, x_1)))
        kept, near_atts = fence(kept, near_atts)
        near_atts.append(swap(kept[1][1], 1))
        atts = [by_token(v) for k in halves for v in (kept[k][0], near_atts[k])]

        block_out, d_mid, d_xg, da0, da1, da2, da3, s_ac, s_scale2, s_tc, s_gain2, w_mid = middle_one(x_one, gates, atts)
        near_att = [swap(by_sample(v), 1) for v in (da1, da3)]
        near_att, w_mid = fence(near_att, w_mid)
        mid = lax.psum_scatter(w_mid, "head", scatter_dimension=0, tiled=False)

        dq_0, dkv_0, *db_0 = back_one(kept[0], by_sample(da0), near_att[0])
        db_0, kept_1 = fence(db_0, kept[1])
        keep_a, got_a, keep_b, got_b = db_0[0], across(db_0[1]), db_0[2], across(db_0[3])
        dq_1, dkv_1, *db_1 = back_one(kept_1, by_sample(da2), near_att[1])
        dq_1, db_1, got_a = fence(dq_1, db_1, got_a)
        keep_c, got_c, keep_d = db_1[0], across(db_1[1]), db_1[2]
        zs_a = z_first(keep_a, got_a)
        cut = samples // 2
        back_heads = lambda grads, span, start, full: heads_back(
            meta, blocks, w_q, w_kv, grads, parts, wch=wide, fast=full, span=span, start=start
        )
        near_1, cross_1, far_1, own_1, *start = back_heads([(dq_0, dkv_0), (dq_1, dkv_1)], (0, cut), (), False)
        near_1, cross_1, far_1, start, zs_a, dq_1 = fence(near_1, cross_1, far_1, start, zs_a, dq_1)
        cross_1 = swap(cross_1, 1)
        cross_1, dq_1, got_b = fence(cross_1, dq_1, got_b)
        half_1 = low(far_1, cross_1)
        half_1, dq_1 = fence(half_1, dq_1)
        far_x, near_x = [swap(half_1, 2)], [swap(near_1, 1)]
        zs_b, last_a = z_first(keep_b, got_b), z_second(keep_a, got_a, zs_a)
        near_2, cross_2, far_2, own_2, gb, keep_w, send_w = back_heads(
            [(dq_0, dkv_0), (dq_1, dkv_1)], (cut, samples - cut), start, True
        )
        near_2, cross_2, far_2, send_w, send_d, last_a, zs_b, far_x[0] = fence(
            near_2, cross_2, far_2, send_w, db_1[3], last_a, zs_b, far_x[0]
        )
        cross_2, got_d = swap(cross_2, 1), across(send_d)
        cross_2, got_c = fence(cross_2, got_c)
        far_x.append(swap(low(far_2, cross_2), 2))
        zs_c, last_b = z_first(keep_c, got_c), z_second(keep_b, got_b, zs_b)
        far_x[1], got_d, zs_c, last_b, send_w, mid, near_2 = fence(far_x[1], got_d, zs_c, last_b, send_w, mid, near_2)
        zs_d, last_c = z_first(keep_d, got_d), z_second(keep_c, got_c, zs_c)
        keep_m, got_m = x_step(mid)
        far_w = swap(send_w, 2)
        sums = [low(z_total(keep_a, got_a, zs_a, last_a)), low(z_total(keep_b, got_b, zs_b, last_b))]
        zs_d, last_c, sums, near_2 = fence(zs_d, last_c, sums, near_2)
        near_x.append(swap(near_2, 1))
        sums.append(low(z_total(keep_c, got_c, zs_c, last_c)))
        last_d = z_second(keep_d, got_d, zs_d)
        near_x, sums = fence(near_x, sums)
        grad_single, s_scale1, s_gain1, keep_l, send_l = last(
            meta, (*map(by_token, (own_1, own_2, *near_x, *far_x)), d_xg), single_t, cond_t, d_mid, *weights_one, fast
        )
        last_d, got_m, far_w, keep_l, send_l, s_gain1, s_scale1 = fence(
            last_d, got_m, far_w, keep_l, send_l, s_gain1, s_scale1
        )
        sums.append(low(z_total(keep_d, got_d, zs_d, last_d)))
        far_rows = swap(jnp.stack([v[..., rows:] for v in sums]), 1)
        near_l = swap(send_l, 1)
        z_m = z_first(keep_m, got_m)
        keep_h, got_h = x_step(low(keep_w, far_w))
        others = jnp.concatenate(
            [v.reshape(-1) for v in (s_gain1, s_scale1, *q_sums(gb), s_gain2, s_ac, s_scale2, s_tc)]
        )
        far_rows, near_l, others = fence(far_rows, near_l, others)
        far_l = swap(low(keep_l[1], near_l[1]), 2)
        pair_grads = [jnp.stack([v[..., :rows] for v in sums[2 * k : 2 * k + 2]]) for k in halves]
        pair_grads += [far_rows[:2], far_rows[2:]]
        grad_pair, grad_pair_weight = pair_back(pair_meta, pair_low, pair_inverse, pair_raw, w_pair, pair_grads, **sizes)
        far_l, got_h, z_m, grad_pair_weight = fence(far_l, got_h, z_m, grad_pair_weight)
        late = total_step(jnp.concatenate([grad_pair_weight.reshape(-1), others]), 0)
        keep_l, got_l = x_step(low(keep_l[0], near_l[0], far_l))
        e_m = z_second(keep_m, got_m, z_m)
        z_h = z_first(keep_h, got_h)
        late, got_l, e_m, z_h = fence(late, got_l, e_m, z_h)

        def settle(block):
            size = block.shape[1] // 2
            left, right = block[:, :size], block[:, size:]
            got = swap(jnp.where(first, right, left), 1)
            held = jnp.where(first, left, right)
            return jnp.where(first, held, got), jnp.where(first, got, held)

        late = total_step(late, 1)
        z_l = z_first(keep_l, got_l)
        e_h = z_second(keep_h, got_h, z_h)
        late, z_l, e_h = fence(late, z_l, e_h)
        late = total_step(late, 2)
        e_l = z_second(keep_l, got_l, z_l)
        late, e_l = fence(late, e_l)
        r_scale1, r_shift1 = settle(z_total(keep_l, got_l, z_l, e_l))
        r_heads = z_total(keep_h, got_h, z_h, e_h)
        n, m, half = width // 8, cs // 8, width // 4
        r_mid = z_total(keep_m, got_m, z_m, e_m)
        r_hg, r_hu = r_mid[:n], r_mid[n : 2 * n]
        r_out, r_gate = r_mid[2 * n : 3 * n, :half], r_mid[2 * n : 3 * n, half:]
        r_tc, r_ac = r_mid[3 * n : 3 * n + m, :half], r_mid[3 * n : 3 * n + m, half:]
        r_scale2, r_shift2 = r_mid[3 * n + m : 3 * n + 2 * m, :half], r_mid[3 * n + m : 3 * n + 2 * m, half:]
        r_down = jnp.concatenate([r_mid[3 * n + 2 * m :, :half], r_mid[3 * n + 2 * m :, half:]], axis=0)
        late = total_step(total_step(late, 3), 4)
    else:
        w_heads, b_heads, w_q, w_kv = own_heads(w_query, w_key, w_value, b_query)
        biases = []
        for own in owns:
            gathered = lax.all_gather(own, "samp", axis=0)
            moved = gathered.transpose(1, 2, 0, 3, 4).reshape(complexes, few, chunks, chunk, 2 * rows)
            biases.append([(moved[:, :, i], None) for i in range(chunks)])
        x_one = adapt(single_t, cond_t, *weights_one)
        x_far = swap(x_one, 2)
        blocks = [by_sample(v) for v in (x_one, swap(x_one, 1), x_far, swap(x_far, 1))]
        kept = [attend_one(k, blocks, biases[k]) for k in halves]
        atts = [by_token(v) for k in halves for v in (kept[k][0], swap(kept[k][1], 1))]
        block_out, d_mid, d_xg, da0, da1, da2, da3, s_ac, s_scale2, s_tc, s_gain2, *w_mid = middle_one(x_one, before(x_one, cond_t, cot_t, weights_two), atts)
        head_grads, sums = [], []
        for k, (own, sent) in enumerate(((da0, da1), (da2, da3))):
            dq, dkv, db = back_one(kept[k], by_sample(own), swap(by_sample(sent), 1))
            head_grads.append((dq, dkv))
            moved = db.transpose(1, 2, 0, 3, 4).reshape(complexes, few, devices, columns, 2 * rows)
            sums.append(lax.psum_scatter(moved, "samp", scatter_dimension=2, tiled=False))
        d_near, d_cross, d_far, d_own, gb, gq, gkv = heads_back(
            meta, blocks, w_q, w_kv, head_grads, parts, wch=wide, fast=fast
        )
        far_x = swap(low(d_far, swap(d_cross, 1)), 2)
        grad_single, s_scale1, s_gain1, w_last = last(
            meta, (*(u for v in (d_own, swap(d_near, 1), far_x) for u in jnp.split(flat(v), 2)), d_xg),
            single_t, cond_t, d_mid, *weights_one, fast,
        )
        pair_grads = [v[..., :rows] for v in sums] + [swap(v[..., rows:], 1) for v in sums]
        grad_pair, grad_pair_weight = pair_back(pair_meta, pair_low, pair_inverse, pair_raw, w_pair, pair_grads, **sizes)

        def total_of(stack):
            axis = stack.ndim - 1
            half = lax.psum_scatter(stack.astype(bf16), "head", scatter_dimension=axis, tiled=True).astype(f32)
            return lax.psum_scatter(half, "samp", scatter_dimension=axis - 1, tiled=True)

        grads = [
            jnp.concatenate([gq[k * wide : (k + 1) * wide], gkv[2 * k * wide : 2 * (k + 1) * wide]], axis=0) for k in halves
        ]
        held = jnp.where(part == 0, grads[0], grads[1])
        sent = jnp.where(part == 0, grads[1], grads[0])
        r_heads = add(held, swap(sent.astype(bf16), 2))
        r_heads = lax.psum_scatter(r_heads.T, "samp", scatter_dimension=0, tiled=True)
        (r_hg, r_hu), (r_out, r_gate), (r_tc, r_ac), (r_scale2, r_shift2), r_down = [total_of(v) for v in w_mid]
        r_scale1, r_shift1 = total_of(w_last)
        late = jnp.concatenate(
            [v.reshape(-1) for v in (grad_pair_weight, s_gain1, s_scale1, *q_sums(gb), s_gain2, s_ac, s_scale2, s_tc)]
        )
        late = lax.psum(late, ("samp", "head"))

    cuts = [heads * w_pair.shape[0]]
    for size in (cs, width, width, cs, width, width):
        cuts.append(cuts[-1] + size)
    sum_pair, sum_gain1, sum_scale1, sum_query, sum_gain2, sum_ac, sum_scale2, sum_tc = jnp.split(late, cuts)
    whole = (samples, rows, width)
    return (
        block_out.reshape(whole),
        grad_single.reshape(whole),
        grad_pair,
        sum_gain1,
        r_scale1,
        sum_scale1,
        r_shift1,
        r_heads[:, :wide],
        sum_query,
        r_heads[:, wide : 2 * wide],
        r_heads[:, 2 * wide :],
        r_gate,
        r_out,
        sum_pair.reshape(heads, -1).T,
        r_ac,
        sum_ac,
        sum_gain2,
        r_scale2,
        sum_scale2,
        r_shift2,
        r_hg,
        r_hu,
        r_down,
        r_tc,
        sum_tc,
    )


def solution(mesh):
    placed = (
        P("samp", "head", None),
        P("samp", "head", None),
        P(None, "head", "samp", None),
        P(),
        P("samp"),
        P("samp", "head", None),
        P(),
        P(),
        P(),
        P(),
        P(),
        P(),
        P(),
        P(),
        P(),
        P(),
        P(),
        P(),
        P(),
        P(),
        P(),
        P(),
        P(),
        P(),
        P(),
        P(),
        P(),
        P(),
    )
    return jax.shard_map(
        on_device,
        mesh=mesh,
        in_specs=placed,
        out_specs=(
            P("samp", "head", None),
            P("samp", "head", None),
            P(None, "head", "samp", None),
            P(),
            P("samp", "head"),
            P(),
            P("samp", "head"),
            P("samp", "head"),
            P(),
            P("samp", "head"),
            P("samp", "head"),
            P("samp", "head"),
            P("samp", "head"),
            P(),
            P("samp", "head"),
            P(),
            P(),
            P("samp", "head"),
            P(),
            P("samp", "head"),
            P("samp", "head"),
            P("samp", "head"),
            P("samp", "head"),
            P("samp", "head"),
            P(),
        ),
        check_vma=False,
    )
```

profile of v0, /device:TPU:0, one launch (start us, length us, event | category | flops | bytes accessed | tf_op | source)
XLA Modules:
  0.0 568.1 jit_solution(7243122476980865015)
XLA Ops:
  10.6 16.6 %pair_bias.1 = (bf16[2,192,96,128]{3,2,1,0:T(8,128)(2,1)}, f32[2,24,96,128]{3,2,1,0:T(8,128)}, f32[2,24,96,128]{3,2,1,0:T(8,128)}, bf16[2,4,96,192]{3,2,1,0:T(8,...) custom-call(s32[2]{0:T(128)} %pad_add_fusion.1.meta, ...), custom_call_target="tpu_custom_call" | custom-call | flops 1048576 | bytes 1048576 | tf_op jit(solution)/shard_map/pair_bias/pallas_call | solution.py:445
  32.1 2.9 collective-permute-start.4
  40.4 8.1 %adapt.1.x_ref = bf16[1536,768]{1,0:T(8,128)(2,1)} custom-call(bf16[1536,768]{1,0:T(8,128)(2,1)} %bitcast.121, bf16[1536,384]{1,0:T(8,128)(2,1)} %bitcast.124, bf16[1,384]{1,0:T(2,128)(2,1)} %reshape.279.gain, bf16[384,768]{1,0:T(8,128)(2,1)} %w_scale.7, bf16[1,768]{1,0:T(2,128)(2,1)} %reshape.280.b_scale, bf16[384,768]{1,0:T(8,128)(2,1)} %w_shift.7), custom_call_target="tpu_custom_call" | custom-call | flops 1048576 | bytes 1048576 | tf_op jit(solution)/shard_map/adapt/pallas_call | solution.py:561
  48.5 15.4 %collective-permute-done.2.rest_2_ = bf16[2,4,96,384]{3,2,1,0:T(8,128)(2,1)} collective-permute-done((bf16[2,4,96,384]{3,2,1,0:T(8,128)(2,1)S(1)}, bf16[2,4,96,384]{3,2,1,0:T(8,128)(2,1)}, u32[]{:S(2)}, u32[]{:S(2)}) %collective-permute-start.2) | collective-permute-done | bytes 589856 | tf_op jit(solution)/shard_map/ppermute | solution.py:863
  73.8 19.3 %collective-permute-done.6.rest_2_ = bf16[2,4,96,384]{3,2,1,0:T(8,128)(2,1)} collective-permute-done((bf16[2,4,96,384]{3,2,1,0:T(8,128)(2,1)S(1)}, bf16[2,4,96,384]{3,2,1,0:T(8,128)(2,1)}, u32[]{:S(2)}, u32[]{:S(2)}) %collective-permute-start.6) | collective-permute-done | bytes 589856 | tf_op jit(solution)/shard_map/ppermute | solution.py:863
  93.4 3.3 collective-permute-done.9.rest_5_
  106.2 16.3 %before.1 = (f32[1536,768]{1,0:T(8,128)}, f32[1536,768]{1,0:T(8,128)}, f32[1536,768]{1,0:T(8,128)}, f32[1536,768]{1,0:T(8,128)}, bf16[1536,768]{1,0:T(8,128)(2,1)}, /*index=5*/bf16[1536,1536]{1,0:T(8,128)(2,1)}) custom-call(bf16[1536,768]{1,0:T(8,128)(2,1)} %adapt.1.x_ref, bf16[1536,384]{1,0:T(8,128)(2,1)} %bitcast.125, bf16[1536,768]{1,0:T(8,128)(2,1)} %bitcast.128, ...), custom_call_target="tpu_custom_call" | custom-call | flops 1048576 | bytes 1048576 | tf_op jit(solution)/shard_map/before/pallas_call | solution.py:604
  135.0 29.6 %attend.2 = (bf16[8,192,192]{2,1,0:T(8,128)(2,1)}, bf16[8,192,192]{2,1,0:T(8,128)(2,1)}, bf16[8,4,768,384]{3,2,1,0:T(8,128)(2,1)}, bf16[8,192,384]{2,1,0:T(8,128...) custom-call(s32[22]{0:T(128)} %concatenate.39.meta, ...), custom_call_target="tpu_custom_call" | custom-call | flops 1048576 | bytes 1048576 | tf_op jit(solution)/shard_map/attend/pallas_call | solution.py:135
  166.5 30.0 %attend.3 = (bf16[8,192,192]{2,1,0:T(8,128)(2,1)}, bf16[8,192,192]{2,1,0:T(8,128)(2,1)}, bf16[8,4,768,384]{3,2,1,0:T(8,128)(2,1)}, bf16[8,192,384]{2,1,0:T(8,128...) custom-call(s32[22]{0:T(128)} %concatenate.39.meta, ...), custom_call_target="tpu_custom_call" | custom-call | flops 1048576 | bytes 1048576 | tf_op jit(solution)/shard_map/attend/pallas_call | solution.py:135
  200.0 74.9 %middle.1 = (bf16[1536,768]{1,0:T(8,128)(2,1)}, f32[1536,768]{1,0:T(8,128)}, bf16[1536,768]{1,0:T(8,128)(2,1)}, bf16[1536,192]{1,0:T(8,128)(2,1)}, bf16[1536,192...) custom-call(s32[22]{0:T(128)} %concatenate.39.meta, ...), custom_call_target="tpu_custom_call" | custom-call | flops 1048576 | bytes 1048576 | tf_op jit(solution)/shard_map/middle/pallas_call | solution.py:755
  279.5 27.7 %attend_back.2 = (bf16[8,192,384]{2,1,0:T(8,128)(2,1)}, bf16[8,384,768]{2,1,0:T(8,128)(2,1)}, bf16[4,4,96,384]{3,2,1,0:T(8,128)(2,1)}, bf16[4,4,96,384]{3,2,1,0:...) custom-call(s32[22]{0:T(128)} %concatenate.39.meta, ...), custom_call_target="tpu_custom_call" | custom-call | flops 1048576 | bytes 1048576 | tf_op jit(solution)/shard_map/attend_back/pallas_call | solution.py:256
  308.5 26.6 %attend_back.3 = (bf16[8,192,384]{2,1,0:T(8,128)(2,1)}, bf16[8,384,768]{2,1,0:T(8,128)(2,1)}, bf16[4,4,96,384]{3,2,1,0:T(8,128)(2,1)}, bf16[4,4,96,384]{3,2,1,0:...) custom-call(s32[22]{0:T(128)} %concatenate.39.meta, ...), custom_call_target="tpu_custom_call" | custom-call | flops 1048576 | bytes 1048576 | tf_op jit(solution)/shard_map/attend_back/pallas_call | solution.py:256
  337.4 15.5 %heads_back.2 = (bf16[4,192,768]{2,1,0:T(8,128)(2,1)}, bf16[4,192,768]{2,1,0:T(8,128)(2,1)}, bf16[4,192,768]{2,1,0:T(8,128)(2,1)}, bf16[4,192,768]{2,1,0:T(8,128...) custom-call(s32[22]{0:T(128)} %concatenate.39.meta, bf16[8,192,768]{2,1,0:T(8,128)(2,1)} %bitcast.119, ...), custom_call_target="tpu_custom_call" | custom-call | flops 1048576 | bytes 1048576 | tf_op jit(solution)/shard_map/heads_back/pallas_call | solution.py:350
  353.8 10.3 %collective-permute-done.25 = bf16[4,4,96,384]{3,2,1,0:T(8,128)(2,1)} collective-permute-done((bf16[4,4,96,384]{3,2,1,0:T(8,128)(2,1)}, bf16[4,4,96,384]{3,2,1,0:T(8,128)(2,1)}, u32[]{:S(2)}, u32[]{:S(2)}) %collective-permute-start.25) | collective-permute-done | bytes 1179680 | tf_op jit(solution)/shard_map/ppermute | solution.py:859
  372.3 19.2 %heads_back.3 = (bf16[4,192,768]{2,1,0:T(8,128)(2,1)}, bf16[4,192,768]{2,1,0:T(8,128)(2,1)}, bf16[4,192,768]{2,1,0:T(8,128)(2,1)}, bf16[4,192,768]{2,1,0:T(8,128...) custom-call(s32[22]{0:T(128)} %concatenate.39.meta, ...), custom_call_target="tpu_custom_call" | custom-call | flops 1048576 | bytes 1048576 | tf_op jit(solution)/shard_map/heads_back/pallas_call | solution.py:350
  394.5 4.3 collective-permute-done.31
  406.1 12.8 %collective-permute-done.35 = bf16[4,96,384]{2,1,0:T(8,128)(2,1)S(1)} collective-permute-done((bf16[4,96,384]{2,1,0:T(8,128)(2,1)S(1)}, bf16[4,96,384]{2,1,0:T(8,128)(2,1)S(1)}, u32[]{:S(2)}, u32[]{:S(2)}) %collective-permute-start.35) | collective-permute-done | bytes 294944 | tf_op jit(solution)/shard_map/ppermute | solution.py:863
  418.9 4.1 collective-permute-done.33
  438.6 7.2 %collective-permute-done.37 = bf16[4,96,384]{2,1,0:T(8,128)(2,1)S(1)} collective-permute-done((bf16[4,96,384]{2,1,0:T(8,128)(2,1)S(1)}, bf16[4,96,384]{2,1,0:T(8,128)(2,1)S(1)}, u32[]{:S(2)}, u32[]{:S(2)}) %collective-permute-start.37) | collective-permute-done | bytes 294944 | tf_op jit(solution)/shard_map/ppermute | solution.py:863
  457.2 17.5 %last.1 = (f32[1536,768]{1,0:T(8,128)}, f32[1,768]{1,0:T(1,128)}, f32[1,384]{1,0:T(1,128)}, bf16[2,8,48,384]{3,2,1,0:T(8,128)(2,1)}, bf16[2,8,48,384]{3,2,1,0:T(8,128)(2,1)}) custom-call(s32[22]{0:T(128)} %concatenate.39.meta, bf16[768,768]{1,0:T(8,128)(2,1)} %bitcast.136, bf16[768,768]{1,0:T(8,128)(2,1)} %bitcast.137, bf16[768,768]{1,0:T(8,128)(2,1)} %bitcast.41.d2, ...), custom_call_target="tpu_custom_call" | custom-call | flops 1048576 | bytes 1048576 | tf_op jit(solution)/shard_map/last/pallas_call | solution.py:835
  493.9 18.5 %pair_back.1 = (f32[2,192,96,128]{3,2,1,0:T(8,128)}, f32[16,128]{1,0:T(8,128)}) custom-call(s32[2]{0:T(128)} %pad_add_fusion.1.meta, bf16[2,192,96,128]{3,2,1,0:T(8,128)(2,1)} %get-tuple-element.425.low_ref, f32[2,24,96,128]{3,2,1,0:T(8,128)} %get-tuple-element.426.inv_ref, f32[2,24,96,128]{3,2,1,0:T(8,128)} %get-tuple-element.427.raw_ref, ...), custom_call_target="tpu_custom_call" | custom-call | flops 1048576 | bytes 1048576 | tf_op jit(solution)/shard_map/pair_back/pallas_call | solution.py:524
  517.6 6.0 %collective-permute-done.48 = bf16[4,48,384]{2,1,0:T(8,128)(2,1)S(1)} collective-permute-done((bf16[4,48,384]{2,1,0:T(8,128)(2,1)S(1)}, bf16[4,48,384]{2,1,0:T(8,128)(2,1)S(1)}, u32[]{:S(2)}, u32[]{:S(2)}) %collective-permute-start.48) | collective-permute-done | bytes 147488 | tf_op jit(solution)/shard_map/ppermute | solution.py:859
  523.6 10.5 %collective-permute-done.49 = bf16[480,384]{1,0:T(8,128)(2,1)S(1)} collective-permute-done((bf16[480,384]{1,0:T(8,128)(2,1)S(1)}, bf16[480,384]{1,0:T(8,128)(2,1)S(1)}, u32[]{:S(2)}, u32[]{:S(2)}) %collective-permute-start.49) | collective-permute-done | bytes 368672 | tf_op jit(solution)/shard_map/ppermute | solution.py:863
  541.9 2.9 collective-permute-done.51
  (324 shorter events, 153.1 us)
Async XLA Ops:
  7.2 418.6 %reduce-scatter.2.cloned.1.call-start = ((), (), s32[]{:S(2)}) async-start(), calls=%async_computation.1 | async-start | bytes 14745600 | tf_op jit(solution)/shard_map/reduce_scatter | solution.py:1054
  32.1 32.0 %collective-permute-start.4 = (bf16[2,2,4,96,384]{4,3,2,1,0:T(8,128)(2,1)S(1)}, bf16[2,2,4,96,384]{4,3,2,1,0:T(8,128)(2,1)S(1)}, u32[]{:S(2)}, u32[]{:S(2)}) collective-permute-start(bf16[2,2,4,96,384]{4,3,2,1,0:T(8,128)(2,1)S(1)} %pad_maximum_fusion), channel_id=1, source_target_pairs={{0,4},{4,0},{8,12},{12,8},{16,20},{20,16},{24,28},{28,24},{1,5},{5... | collective-permute-start | bytes 3538952 | tf_op jit(solution)/shard_map/ppermute | solution.py:859
  35.1 28.8 %collective-permute-start.2 = (bf16[2,4,96,384]{3,2,1,0:T(8,128)(2,1)S(1)}, bf16[2,4,96,384]{3,2,1,0:T(8,128)(2,1)}, u32[]{:S(2)}, u32[]{:S(2)}) collective-permute-start(bf16[2,4,96,384]{3,2,1,0:T(8,128)(2,1)S(1)} %pad_maximum_fusion.5.rest_0_), channel_id=1, source_target_pairs={{0,16},{4,20},{8,24},{12,28},{16,0},{20,4},{24,8},{28,12},{1,17},{... | collective-permute-start | bytes 1769480 | tf_op jit(solution)/shard_map/ppermute | solution.py:863
  37.6 26.4 %collective-permute-start.3 = (bf16[2,4,96,384]{3,2,1,0:T(8,128)(2,1)S(1)}, bf16[2,4,96,384]{3,2,1,0:T(8,128)(2,1)}, u32[]{:S(2)}, u32[]{:S(2)}) collective-permute-start(bf16[2,4,96,384]{3,2,1,0:T(8,128)(2,1)S(1)} %pad_maximum_fusion.5.rest_0_), channel_id=1, source_target_pairs={{0,8},{4,12},{8,0},{12,4},{16,24},{20,28},{24,16},{28,20},{1,9},{5... | collective-permute-start | bytes 1769480 | tf_op jit(solution)/shard_map/ppermute | solution.py:863
  64.1 61.8 %collective-permute-start.5 = (bf16[1536,768]{1,0:T(8,128)(2,1)}, bf16[1536,768]{1,0:T(8,128)(2,1)}, u32[]{:S(2)}, u32[]{:S(2)}) collective-permute-start(bf16[1536,768]{1,0:T(8,128)(2,1)} %adapt.1.x_ref), channel_id=1, source_target_pairs={{0,2},{1,3},{2,0},{3,1},{4,6},{5,7},{6,4},{7,5},{8,10},{9,11},{10,... | collective-permute-start | bytes 7077896 | tf_op jit(solution)/shard_map/ppermute | solution.py:855
  65.6 27.5 %collective-permute-start.6 = (bf16[2,4,96,384]{3,2,1,0:T(8,128)(2,1)S(1)}, bf16[2,4,96,384]{3,2,1,0:T(8,128)(2,1)}, u32[]{:S(2)}, u32[]{:S(2)}) collective-permute-start(bf16[2,4,96,384]{3,2,1,0:T(8,128)(2,1)S(1)} %pad_maximum_fusion.6.rest_0_), channel_id=1, source_target_pairs={{0,16},{4,20},{8,24},{12,28},{16,0},{20,4},{24,8},{28,12},{1,17},{... | collective-permute-start | bytes 1769480 | tf_op jit(solution)/shard_map/ppermute | solution.py:863
  66.9 26.5 %collective-permute-start.7 = (bf16[2,4,96,384]{3,2,1,0:T(8,128)(2,1)}, bf16[2,4,96,384]{3,2,1,0:T(8,128)(2,1)}, u32[]{:S(2)}, u32[]{:S(2)}) collective-permute-start(bf16[2,4,96,384]{3,2,1,0:T(8,128)(2,1)} %collective-permute-done.2.rest_2_), channel_id=1, source_target_pairs={{0,8},{4,12},{8,0},{12,4},{16,24},{20,28},{24,16},{28,20},{1,9},{5... | collective-permute-start | bytes 1769480 | tf_op jit(solution)/shard_map/ppermute | solution.py:863
  70.0 26.7 %collective-permute-start.9 = (bf16[2,4,96,384]{3,2,1,0:T(8,128)(2,1)}, bf16[2,4,96,384]{3,2,1,0:T(8,128)(2,1)S(1)}, u32[]{:S(2)}, u32[]{:S(2)}) collective-permute-start(bf16[2,4,96,384]{3,2,1,0:T(8,128)(2,1)} %collective-permute-done.3.rest_4_), channel_id=1, source_target_pairs={{0,4},{4,0},{8,12},{12,8},{16,20},{20,16},{24,28},{28,24},{1,5},{5... | collective-permute-start | bytes 1769480 | tf_op jit(solution)/shard_map/ppermute | solution.py:859
  96.7 29.1 %collective-permute-start.11 = (bf16[2,4,96,384]{3,2,1,0:T(8,128)(2,1)}, bf16[2,4,96,384]{3,2,1,0:T(8,128)(2,1)}, u32[]{:S(2)}, u32[]{:S(2)}) collective-permute-start(bf16[2,4,96,384]{3,2,1,0:T(8,128)(2,1)} %collective-permute-done.6.rest_2_), channel_id=1, source_target_pairs={{0,4},{4,0},{8,12},{12,8},{16,20},{20,16},{24,28},{28,24},{1,5},{5... | collective-permute-start | bytes 1769480 | tf_op jit(solution)/shard_map/ppermute | solution.py:859
  97.5 28.3 %collective-permute-start.13 = (bf16[2,4,96,384]{3,2,1,0:T(8,128)(2,1)}, bf16[2,4,96,384]{3,2,1,0:T(8,128)(2,1)}, u32[]{:S(2)}, u32[]{:S(2)}) collective-permute-start(bf16[2,4,96,384]{3,2,1,0:T(8,128)(2,1)} %collective-permute-done.6.rest_2_), channel_id=1, source_target_pairs={{0,8},{4,12},{8,0},{12,4},{16,24},{20,28},{24,16},{28,20},{1,9},{5... | collective-permute-start | bytes 1769480 | tf_op jit(solution)/shard_map/ppermute | solution.py:863
  99.4 26.4 %collective-permute-start.10 = (bf16[2,4,96,384]{3,2,1,0:T(8,128)(2,1)}, bf16[2,4,96,384]{3,2,1,0:T(8,128)(2,1)}, u32[]{:S(2)}, u32[]{:S(2)}) collective-permute-start(bf16[2,4,96,384]{3,2,1,0:T(8,128)(2,1)} %collective-permute-done.7.rest_6_), channel_id=1, source_target_pairs={{0,4},{4,0},{8,12},{12,8},{16,20},{20,16},{24,28},{28,24},{1,5},{5... | collective-permute-start | bytes 1769480 | tf_op jit(solution)/shard_map/ppermute | solution.py:859
  127.3 37.4 %collective-permute-start.16 = (bf16[2,4,96,384]{3,2,1,0:T(8,128)(2,1)}, bf16[2,4,96,384]{3,2,1,0:T(8,128)(2,1)S(1)}, u32[]{:S(2)}, u32[]{:S(2)}) collective-permute-start(bf16[2,4,96,384]{3,2,1,0:T(8,128)(2,1)} %collective-permute-done.12.rest_4_), channel_id=1, source_target_pairs={{0,4},{4,0},{8,12},{12,8},{16,20},{20,16},{24,28},{28,24},{1,5},{5... | collective-permute-start | bytes 1769480 | tf_op jit(solution)/shard_map/ppermute | solution.py:859
  128.1 36.6 %collective-permute-start.17 = (bf16[2,4,96,384]{3,2,1,0:T(8,128)(2,1)}, bf16[2,4,96,384]{3,2,1,0:T(8,128)(2,1)S(1)}, u32[]{:S(2)}, u32[]{:S(2)}) collective-permute-start(bf16[2,4,96,384]{3,2,1,0:T(8,128)(2,1)} %collective-permute-done.13.rest_6_), channel_id=1, source_target_pairs={{0,4},{4,0},{8,12},{12,8},{16,20},{20,16},{24,28},{28,24},{1,5},{5... | collective-permute-start | bytes 1769480 | tf_op jit(solution)/shard_map/ppermute | solution.py:859
  165.6 30.9 %collective-permute-start.18 = (bf16[8,192,192]{2,1,0:T(8,128)(2,1)}, bf16[8,192,192]{2,1,0:T(8,128)(2,1)S(1)}, u32[]{:S(2)}, u32[]{:S(2)}) collective-permute-start(bf16[8,192,192]{2,1,0:T(8,128)(2,1)} %get-tuple-element.333.o1), channel_id=1, source_target_pairs={{0,1},{1,0},{2,3},{3,2},{4,5},{5,4},{6,7},{7,6},{8,9},{9,8},{10,11... | collective-permute-start | bytes 1769480 | tf_op jit(solution)/shard_map/ppermute | solution.py:855
  307.1 28.5 %collective-permute-start.22 = (bf16[4,4,96,384]{3,2,1,0:T(8,128)(2,1)}, bf16[4,4,96,384]{3,2,1,0:T(8,128)(2,1)S(1)}, u32[]{:S(2)}, u32[]{:S(2)}) collective-permute-start(bf16[4,4,96,384]{3,2,1,0:T(8,128)(2,1)} %get-tuple-element.363), channel_id=1, source_target_pairs={{0,4},{4,0},{8,12},{12,8},{16,20},{20,16},{24,28},{28,24},{1,5},{5... | collective-permute-start | bytes 3538952 | tf_op jit(solution)/shard_map/ppermute | solution.py:859
  336.5 27.6 %collective-permute-start.25 = (bf16[4,4,96,384]{3,2,1,0:T(8,128)(2,1)}, bf16[4,4,96,384]{3,2,1,0:T(8,128)(2,1)}, u32[]{:S(2)}, u32[]{:S(2)}) collective-permute-start(bf16[4,4,96,384]{3,2,1,0:T(8,128)(2,1)} %get-tuple-element.379), channel_id=1, source_target_pairs={{0,4},{4,0},{8,12},{12,8},{16,20},{20,16},{24,28},{28,24},{1,5},{5... | collective-permute-start | bytes 3538952 | tf_op jit(solution)/shard_map/ppermute | solution.py:859
  365.7 27.3 %collective-permute-start.29 = (bf16[4,192,768]{2,1,0:T(8,128)(2,1)S(1)}, bf16[4,192,768]{2,1,0:T(8,128)(2,1)}, u32[]{:S(2)}, u32[]{:S(2)}) collective-permute-start(bf16[4,192,768]{2,1,0:T(8,128)(2,1)S(1)} %add_convert_fusion.1), channel_id=1, source_target_pairs={{0,2},{1,3},{2,0},{3,1},{4,6},{5,7},{6,4},{7,5},{8,10},{9,11},{10,... | collective-permute-start | bytes 3538952 | tf_op jit(solution)/shard_map/ppermute | solution.py:855
  371.5 27.3 %collective-permute-start.31 = (bf16[4,4,96,384]{3,2,1,0:T(8,128)(2,1)}, bf16[4,4,96,384]{3,2,1,0:T(8,128)(2,1)S(1)}, u32[]{:S(2)}, u32[]{:S(2)}) collective-permute-start(bf16[4,4,96,384]{3,2,1,0:T(8,128)(2,1)} %get-tuple-element.400), channel_id=1, source_target_pairs={{0,4},{4,0},{8,12},{12,8},{16,20},{20,16},{24,28},{28,24},{1,5},{5... | collective-permute-start | bytes 3538952 | tf_op jit(solution)/shard_map/ppermute | solution.py:859
  393.0 30.0 %collective-permute-start.33 = (bf16[4,4,96,384]{3,2,1,0:T(8,128)(2,1)}, bf16[4,4,96,384]{3,2,1,0:T(8,128)(2,1)}, u32[]{:S(2)}, u32[]{:S(2)}) collective-permute-start(bf16[4,4,96,384]{3,2,1,0:T(8,128)(2,1)} %get-tuple-element.402), channel_id=1, source_target_pairs={{0,4},{4,0},{8,12},{12,8},{16,20},{20,16},{24,28},{28,24},{1,5},{5... | collective-permute-start | bytes 3538952 | tf_op jit(solution)/shard_map/ppermute | solution.py:859
  406.1 51.1 %collective-permute-start.26 = (bf16[4,192,768]{2,1,0:T(8,128)(2,1)}, bf16[4,192,768]{2,1,0:T(8,128)(2,1)}, u32[]{:S(2)}, u32[]{:S(2)}) collective-permute-start(bf16[4,192,768]{2,1,0:T(8,128)(2,1)} %get-tuple-element.387), channel_id=1, source_target_pairs={{0,1},{1,0},{2,3},{3,2},{4,5},{5,4},{6,7},{7,6},{8,9},{9,8},{10,11... | collective-permute-start | bytes 3538952 | tf_op jit(solution)/shard_map/ppermute | solution.py:855
  433.8 40.9 %collective-permute-start.40 = (bf16[4,480,384]{2,1,0:T(8,128)(2,1)}, bf16[4,480,384]{2,1,0:T(8,128)(2,1)}, u32[]{:S(2)}, u32[]{:S(2)}) collective-permute-start(bf16[4,480,384]{2,1,0:T(8,128)(2,1)} %slice.329), channel_id=1, source_target_pairs={{0,4},{4,0},{8,12},{12,8},{16,20},{20,16},{24,28},{28,24},{1,5},{5... | collective-permute-start | bytes 4423688 | tf_op jit(solution)/shard_map/ppermute | solution.py:859
  447.4 27.3 %collective-permute-start.41 = (bf16[8,96,576]{2,1,0:T(8,128)(2,1)}, bf16[8,96,576]{2,1,0:T(8,128)(2,1)}, u32[]{:S(2)}, u32[]{:S(2)}) collective-permute-start(bf16[8,96,576]{2,1,0:T(8,128)(2,1)} %get-tuple-element.433), channel_id=1, source_target_pairs={{0,2},{1,3},{2,0},{3,1},{4,6},{5,7},{6,4},{7,5},{8,10},{9,11},{10,... | collective-permute-start | bytes 2654216 | tf_op jit(solution)/shard_map/ppermute | solution.py:855
  481.6 30.9 %collective-permute-start.46 = (bf16[2,480,384]{2,1,0:T(8,128)(2,1)}, bf16[2,480,384]{2,1,0:T(8,128)(2,1)S(1)}, u32[]{:S(2)}, u32[]{:S(2)}) collective-permute-start(bf16[2,480,384]{2,1,0:T(8,128)(2,1)} %add_convert_fusion.3), channel_id=1, source_target_pairs={{0,8},{4,12},{8,0},{12,4},{16,24},{20,28},{24,16},{28,20},{1,9},{5... | collective-permute-start | bytes 2211848 | tf_op jit(solution)/shard_map/ppermute | solution.py:863
  485.0 27.5 %collective-permute-start.45 = (bf16[4,96,576]{2,1,0:T(8,128)(2,1)}, bf16[4,96,576]{2,1,0:T(8,128)(2,1)}, u32[]{:S(2)}, u32[]{:S(2)}) collective-permute-start(bf16[4,96,576]{2,1,0:T(8,128)(2,1)} %slice.386), channel_id=1, source_target_pairs={{0,4},{4,0},{8,12},{12,8},{16,20},{20,16},{24,28},{28,24},{1,5},{5... | collective-permute-start | bytes 1327112 | tf_op jit(solution)/shard_map/ppermute | solution.py:859
  (92 other events, 907.4 us)
Sparse Core Ops, SparseCore 0:
  278.7 91.0 reduce-scatter.1
where the time goes:
time: 578 us; the launch traced here: 568 us
  Pallas kernels  301 us (52%)
  waiting for transfers between devices  118 us (20%)
  starting transfers between devices  57.6 us (10%)
  other arithmetic  47.1 us (8%)
  local copies, waits for them, and re-layouts  29 us (5%)
  between operations  15.3 us (3%)
    pallas_call x1, Pallas kernels, middle(): pl.pallas_call(functools.partial(middle_kernel, tiles=tiles, fast=fast),...  74.9 us
    ppermute x22, waiting for transfers between devices, slot(): return lax.ppermute(value, 'samp', [(i, i ^ 2 * bit) for i in range(8)])  70.6 us
    pallas_call x2, Pallas kernels, attend(): pl.pallas_call(kern, grid_spec=pltpu.PrefetchScalarGridSpec(num_scalar_pr...  59.6 us
    pallas_call x2, Pallas kernels, attend_back(): pl.pallas_call(kern, grid_spec=pltpu.PrefetchScalarGridSpec(num_scalar_pr...  54.2 us
    pallas_call x2, Pallas kernels, heads_back(): pl.pallas_call(functools.partial(heads_back_kernel, parts=parts, rows=row...  34.8 us
    ppermute x15, waiting for transfers between devices, across(): return lax.ppermute(value, 'samp', [(i, i ^ 1) for i in range(8)])  31 us
    ppermute x22, starting transfers between devices, slot(): return lax.ppermute(value, 'samp', [(i, i ^ 2 * bit) for i in range(8)])  30.1 us
    convert_element_type x23, other arithmetic, low(): return add(*terms).astype(bf16)  27.7 us
  transfers between devices with their start and end apart: 60, of which 29 were waited for; matrix products, arithmetic and copies ran while one was open for 9% of the time, Pallas kernels for 37%

commit v1 on v0

--- a/solution.py
+++ b/solution.py
@@ -13,7 +13,7 @@
 fill_value = -1e30
 LOG2E = math.log2(math.e)
 VMEM_BYTES = 60 << 20
-PAIR_LINES = (8, 16, 24, 32, 64)
+PAIR_LINES = (8, 16, 24, 32, 64, 192)
 NN, NT, TN = ((1,), (0,)), ((1,), (1,)), ((0,), (0,))
 
 
@@ -1116,7 +1116,7 @@
         keep_l, got_l = x_step(low(keep_l[0], near_l[0], far_l))
         e_m = z_second(keep_m, got_m, z_m)
         z_h = z_first(keep_h, got_h)
-        late, got_l, e_m, z_h = fence(late, got_l, e_m, z_h)
+        late, got_l = fence(late, got_l)
 
         def settle(block):
             size = block.shape[1] // 2
@@ -1127,11 +1127,11 @@
 
         late = total_step(late, 1)
         z_l = z_first(keep_l, got_l)
-        e_h = z_second(keep_h, got_h, z_h)
-        late, z_l, e_h = fence(late, z_l, e_h)
+        late, z_l, z_h, e_m = fence(late, z_l, z_h, e_m)
         late = total_step(late, 2)
         e_l = z_second(keep_l, got_l, z_l)
-        late, e_l = fence(late, e_l)
+        e_h = z_second(keep_h, got_h, z_h)
+        late, e_l, e_h = fence(late, e_l, e_h)
         r_scale1, r_shift1 = settle(z_total(keep_l, got_l, z_l, e_l))
         r_heads = z_total(keep_h, got_h, z_h, e_h)
         n, m, half = width // 8, cs // 8, width // 4

time: 578 us -> 574 us (level)
  transfers between devices with their start and end apart: 60 -> 60, of which waited for: 29 -> 27; matrix products, arithmetic and copies ran while one was open for 9% -> 9% of each run, Pallas kernels for 37% -> 37%
where the time goes in v1:
time: 574 us; the launch traced here: 564 us
  Pallas kernels  298 us (52%)
  waiting for transfers between devices  118 us (21%)
  starting transfers between devices  56.6 us (10%)
  other arithmetic  47.1 us (8%)
  local copies, waits for them, and re-layouts  29 us (5%)
  between operations  15.3 us (3%)
    pallas_call x1, Pallas kernels, middle(): pl.pallas_call(functools.partial(middle_kernel, tiles=tiles, fast=fast),...  74.9 us
    ppermute x22, waiting for transfers between devices, slot(): return lax.ppermute(value, 'samp', [(i, i ^ 2 * bit) for i in range(8)])  68.5 us
    pallas_call x2, Pallas kernels, attend(): pl.pallas_call(kern, grid_spec=pltpu.PrefetchScalarGridSpec(num_scalar_pr...  59.6 us
    pallas_call x2, Pallas kernels, attend_back(): pl.pallas_call(kern, grid_spec=pltpu.PrefetchScalarGridSpec(num_scalar_pr...  54.2 us
    pallas_call x2, Pallas kernels, heads_back(): pl.pallas_call(functools.partial(heads_back_kernel, parts=parts, rows=row...  34.8 us
    ppermute x15, waiting for transfers between devices, across(): return lax.ppermute(value, 'samp', [(i, i ^ 1) for i in range(8)])  31.4 us
    ppermute x22, starting transfers between devices, slot(): return lax.ppermute(value, 'samp', [(i, i ^ 2 * bit) for i in range(8)])  29.4 us
    convert_element_type x23, other arithmetic, low(): return add(*terms).astype(bf16)  27.7 us
  transfers between devices with their start and end apart: 60, of which 27 were waited for; matrix products, arithmetic and copies ran while one was open for 9% of the time, Pallas kernels for 37%

profile of v1, /device:TPU:0, one launch (start us, length us, event | category | flops | bytes accessed | tf_op | source)
XLA Modules:
  0.0 564.1 jit_solution(10216257155219456323)
XLA Ops:
  10.6 15.8 %pair_bias.1 = (bf16[2,192,96,128]{3,2,1,0:T(8,128)(2,1)}, f32[2,24,96,128]{3,2,1,0:T(8,128)}, f32[2,24,96,128]{3,2,1,0:T(8,128)}, bf16[2,4,96,192]{3,2,1,0:T(8,...) custom-call(s32[2]{0:T(128)} %pad_add_fusion.1.meta, ...), custom_call_target="tpu_custom_call" | custom-call | flops 1048576 | bytes 1048576 | tf_op jit(solution)/shard_map/pair_bias/pallas_call | solution.py:445
  39.6 8.1 %adapt.1.x_ref = bf16[1536,768]{1,0:T(8,128)(2,1)} custom-call(bf16[1536,768]{1,0:T(8,128)(2,1)} %bitcast.121, bf16[1536,384]{1,0:T(8,128)(2,1)} %bitcast.124, bf16[1,384]{1,0:T(2,128)(2,1)} %reshape.279.gain, bf16[384,768]{1,0:T(8,128)(2,1)} %w_scale.7, bf16[1,768]{1,0:T(2,128)(2,1)} %reshape.280.b_scale, bf16[384,768]{1,0:T(8,128)(2,1)} %w_shift.7), custom_call_target="tpu_custom_call" | custom-call | flops 1048576 | bytes 1048576 | tf_op jit(solution)/shard_map/adapt/pallas_call | solution.py:561
  47.7 15.4 %collective-permute-done.2.rest_2_ = bf16[2,4,96,384]{3,2,1,0:T(8,128)(2,1)} collective-permute-done((bf16[2,4,96,384]{3,2,1,0:T(8,128)(2,1)S(1)}, bf16[2,4,96,384]{3,2,1,0:T(8,128)(2,1)}, u32[]{:S(2)}, u32[]{:S(2)}) %collective-permute-start.2) | collective-permute-done | bytes 589856 | tf_op jit(solution)/shard_map/ppermute | solution.py:863
  73.0 19.3 %collective-permute-done.6.rest_2_ = bf16[2,4,96,384]{3,2,1,0:T(8,128)(2,1)} collective-permute-done((bf16[2,4,96,384]{3,2,1,0:T(8,128)(2,1)S(1)}, bf16[2,4,96,384]{3,2,1,0:T(8,128)(2,1)}, u32[]{:S(2)}, u32[]{:S(2)}) %collective-permute-start.6) | collective-permute-done | bytes 589856 | tf_op jit(solution)/shard_map/ppermute | solution.py:863
  92.6 3.3 collective-permute-done.9.rest_5_
  105.4 16.3 %before.1 = (f32[1536,768]{1,0:T(8,128)}, f32[1536,768]{1,0:T(8,128)}, f32[1536,768]{1,0:T(8,128)}, f32[1536,768]{1,0:T(8,128)}, bf16[1536,768]{1,0:T(8,128)(2,1)}, /*index=5*/bf16[1536,1536]{1,0:T(8,128)(2,1)}) custom-call(bf16[1536,768]{1,0:T(8,128)(2,1)} %adapt.1.x_ref, bf16[1536,384]{1,0:T(8,128)(2,1)} %bitcast.125, bf16[1536,768]{1,0:T(8,128)(2,1)} %bitcast.128, ...), custom_call_target="tpu_custom_call" | custom-call | flops 1048576 | bytes 1048576 | tf_op jit(solution)/shard_map/before/pallas_call | solution.py:604
  134.2 30.0 %attend.2 = (bf16[8,192,192]{2,1,0:T(8,128)(2,1)}, bf16[8,192,192]{2,1,0:T(8,128)(2,1)}, bf16[8,4,768,384]{3,2,1,0:T(8,128)(2,1)}, bf16[8,192,384]{2,1,0:T(8,128...) custom-call(s32[22]{0:T(128)} %concatenate.39.meta, ...), custom_call_target="tpu_custom_call" | custom-call | flops 1048576 | bytes 1048576 | tf_op jit(solution)/shard_map/attend/pallas_call | solution.py:135
  166.1 29.6 %attend.3 = (bf16[8,192,192]{2,1,0:T(8,128)(2,1)}, bf16[8,192,192]{2,1,0:T(8,128)(2,1)}, bf16[8,4,768,384]{3,2,1,0:T(8,128)(2,1)}, bf16[8,192,384]{2,1,0:T(8,128...) custom-call(s32[22]{0:T(128)} %concatenate.39.meta, ...), custom_call_target="tpu_custom_call" | custom-call | flops 1048576 | bytes 1048576 | tf_op jit(solution)/shard_map/attend/pallas_call | solution.py:135
  199.2 74.9 %middle.1 = (bf16[1536,768]{1,0:T(8,128)(2,1)}, f32[1536,768]{1,0:T(8,128)}, bf16[1536,768]{1,0:T(8,128)(2,1)}, bf16[1536,192]{1,0:T(8,128)(2,1)}, bf16[1536,192...) custom-call(s32[22]{0:T(128)} %concatenate.39.meta, ...), custom_call_target="tpu_custom_call" | custom-call | flops 1048576 | bytes 1048576 | tf_op jit(solution)/shard_map/middle/pallas_call | solution.py:755
  278.7 27.7 %attend_back.2 = (bf16[8,192,384]{2,1,0:T(8,128)(2,1)}, bf16[8,384,768]{2,1,0:T(8,128)(2,1)}, bf16[4,4,96,384]{3,2,1,0:T(8,128)(2,1)}, bf16[4,4,96,384]{3,2,1,0:...) custom-call(s32[22]{0:T(128)} %concatenate.39.meta, ...), custom_call_target="tpu_custom_call" | custom-call | flops 1048576 | bytes 1048576 | tf_op jit(solution)/shard_map/attend_back/pallas_call | solution.py:256
  307.7 26.6 %attend_back.3 = (bf16[8,192,384]{2,1,0:T(8,128)(2,1)}, bf16[8,384,768]{2,1,0:T(8,128)(2,1)}, bf16[4,4,96,384]{3,2,1,0:T(8,128)(2,1)}, bf16[4,4,96,384]{3,2,1,0:...) custom-call(s32[22]{0:T(128)} %concatenate.39.meta, ...), custom_call_target="tpu_custom_call" | custom-call | flops 1048576 | bytes 1048576 | tf_op jit(solution)/shard_map/attend_back/pallas_call | solution.py:256
  336.6 15.5 %heads_back.2 = (bf16[4,192,768]{2,1,0:T(8,128)(2,1)}, bf16[4,192,768]{2,1,0:T(8,128)(2,1)}, bf16[4,192,768]{2,1,0:T(8,128)(2,1)}, bf16[4,192,768]{2,1,0:T(8,128...) custom-call(s32[22]{0:T(128)} %concatenate.39.meta, bf16[8,192,768]{2,1,0:T(8,128)(2,1)} %bitcast.119, ...), custom_call_target="tpu_custom_call" | custom-call | flops 1048576 | bytes 1048576 | tf_op jit(solution)/shard_map/heads_back/pallas_call | solution.py:350
  353.0 10.3 %collective-permute-done.25 = bf16[4,4,96,384]{3,2,1,0:T(8,128)(2,1)} collective-permute-done((bf16[4,4,96,384]{3,2,1,0:T(8,128)(2,1)}, bf16[4,4,96,384]{3,2,1,0:T(8,128)(2,1)}, u32[]{:S(2)}, u32[]{:S(2)}) %collective-permute-start.25) | collective-permute-done | bytes 1179680 | tf_op jit(solution)/shard_map/ppermute | solution.py:859
  371.6 19.2 %heads_back.3 = (bf16[4,192,768]{2,1,0:T(8,128)(2,1)}, bf16[4,192,768]{2,1,0:T(8,128)(2,1)}, bf16[4,192,768]{2,1,0:T(8,128)(2,1)}, bf16[4,192,768]{2,1,0:T(8,128...) custom-call(s32[22]{0:T(128)} %concatenate.39.meta, ...), custom_call_target="tpu_custom_call" | custom-call | flops 1048576 | bytes 1048576 | tf_op jit(solution)/shard_map/heads_back/pallas_call | solution.py:350
  393.7 4.4 collective-permute-done.31
  405.3 12.8 %collective-permute-done.35 = bf16[4,96,384]{2,1,0:T(8,128)(2,1)S(1)} collective-permute-done((bf16[4,96,384]{2,1,0:T(8,128)(2,1)S(1)}, bf16[4,96,384]{2,1,0:T(8,128)(2,1)S(1)}, u32[]{:S(2)}, u32[]{:S(2)}) %collective-permute-start.35) | collective-permute-done | bytes 294944 | tf_op jit(solution)/shard_map/ppermute | solution.py:863
  418.1 4.1 collective-permute-done.33
  437.8 7.0 %collective-permute-done.37 = bf16[4,96,384]{2,1,0:T(8,128)(2,1)S(1)} collective-permute-done((bf16[4,96,384]{2,1,0:T(8,128)(2,1)S(1)}, bf16[4,96,384]{2,1,0:T(8,128)(2,1)S(1)}, u32[]{:S(2)}, u32[]{:S(2)}) %collective-permute-start.37) | collective-permute-done | bytes 294944 | tf_op jit(solution)/shard_map/ppermute | solution.py:863
  456.2 17.5 %last.1 = (f32[1536,768]{1,0:T(8,128)}, f32[1,768]{1,0:T(1,128)}, f32[1,384]{1,0:T(1,128)}, bf16[2,8,48,384]{3,2,1,0:T(8,128)(2,1)}, bf16[2,8,48,384]{3,2,1,0:T(8,128)(2,1)}) custom-call(s32[22]{0:T(128)} %concatenate.39.meta, bf16[768,768]{1,0:T(8,128)(2,1)} %bitcast.136, bf16[768,768]{1,0:T(8,128)(2,1)} %bitcast.137, bf16[768,768]{1,0:T(8,128)(2,1)} %bitcast.41.d2, ...), custom_call_target="tpu_custom_call" | custom-call | flops 1048576 | bytes 1048576 | tf_op jit(solution)/shard_map/last/pallas_call | solution.py:835
  493.1 17.3 %pair_back.1 = (f32[2,192,96,128]{3,2,1,0:T(8,128)}, f32[16,128]{1,0:T(8,128)}) custom-call(s32[2]{0:T(128)} %pad_add_fusion.1.meta, bf16[2,192,96,128]{3,2,1,0:T(8,128)(2,1)} %get-tuple-element.425.low_ref, f32[2,24,96,128]{3,2,1,0:T(8,128)} %get-tuple-element.426.inv_ref, f32[2,24,96,128]{3,2,1,0:T(8,128)} %get-tuple-element.427.raw_ref, ...), custom_call_target="tpu_custom_call" | custom-call | flops 1048576 | bytes 1048576 | tf_op jit(solution)/shard_map/pair_back/pallas_call | solution.py:524
  515.5 6.1 %collective-permute-done.48 = bf16[4,48,384]{2,1,0:T(8,128)(2,1)S(1)} collective-permute-done((bf16[4,48,384]{2,1,0:T(8,128)(2,1)S(1)}, bf16[4,48,384]{2,1,0:T(8,128)(2,1)S(1)}, u32[]{:S(2)}, u32[]{:S(2)}) %collective-permute-start.48) | collective-permute-done | bytes 147488 | tf_op jit(solution)/shard_map/ppermute | solution.py:859
  523.6 3.9 collective-permute-done.49
  527.5 4.1 collective-permute-done.50
  551.8 3.3 collective-permute-done.57
  (324 shorter events, 156.4 us)
Async XLA Ops:
  7.2 417.8 %reduce-scatter.2.cloned.1.call-start = ((), (), s32[]{:S(2)}) async-start(), calls=%async_computation.1 | async-start | bytes 14745600 | tf_op jit(solution)/shard_map/reduce_scatter | solution.py:1054
  31.3 32.0 %collective-permute-start.4 = (bf16[2,2,4,96,384]{4,3,2,1,0:T(8,128)(2,1)S(1)}, bf16[2,2,4,96,384]{4,3,2,1,0:T(8,128)(2,1)S(1)}, u32[]{:S(2)}, u32[]{:S(2)}) collective-permute-start(bf16[2,2,4,96,384]{4,3,2,1,0:T(8,128)(2,1)S(1)} %pad_maximum_fusion), channel_id=1, source_target_pairs={{0,4},{4,0},{8,12},{12,8},{16,20},{20,16},{24,28},{28,24},{1,5},{5... | collective-permute-start | bytes 3538952 | tf_op jit(solution)/shard_map/ppermute | solution.py:859
  34.3 28.8 %collective-permute-start.2 = (bf16[2,4,96,384]{3,2,1,0:T(8,128)(2,1)S(1)}, bf16[2,4,96,384]{3,2,1,0:T(8,128)(2,1)}, u32[]{:S(2)}, u32[]{:S(2)}) collective-permute-start(bf16[2,4,96,384]{3,2,1,0:T(8,128)(2,1)S(1)} %pad_maximum_fusion.5.rest_0_), channel_id=1, source_target_pairs={{0,16},{4,20},{8,24},{12,28},{16,0},{20,4},{24,8},{28,12},{1,17},{... | collective-permute-start | bytes 1769480 | tf_op jit(solution)/shard_map/ppermute | solution.py:863
  36.9 26.4 %collective-permute-start.3 = (bf16[2,4,96,384]{3,2,1,0:T(8,128)(2,1)S(1)}, bf16[2,4,96,384]{3,2,1,0:T(8,128)(2,1)}, u32[]{:S(2)}, u32[]{:S(2)}) collective-permute-start(bf16[2,4,96,384]{3,2,1,0:T(8,128)(2,1)S(1)} %pad_maximum_fusion.5.rest_0_), channel_id=1, source_target_pairs={{0,8},{4,12},{8,0},{12,4},{16,24},{20,28},{24,16},{28,20},{1,9},{5... | collective-permute-start | bytes 1769480 | tf_op jit(solution)/shard_map/ppermute | solution.py:863
  63.3 61.8 %collective-permute-start.5 = (bf16[1536,768]{1,0:T(8,128)(2,1)}, bf16[1536,768]{1,0:T(8,128)(2,1)}, u32[]{:S(2)}, u32[]{:S(2)}) collective-permute-start(bf16[1536,768]{1,0:T(8,128)(2,1)} %adapt.1.x_ref), channel_id=1, source_target_pairs={{0,2},{1,3},{2,0},{3,1},{4,6},{5,7},{6,4},{7,5},{8,10},{9,11},{10,... | collective-permute-start | bytes 7077896 | tf_op jit(solution)/shard_map/ppermute | solution.py:855
  64.8 27.5 %collective-permute-start.6 = (bf16[2,4,96,384]{3,2,1,0:T(8,128)(2,1)S(1)}, bf16[2,4,96,384]{3,2,1,0:T(8,128)(2,1)}, u32[]{:S(2)}, u32[]{:S(2)}) collective-permute-start(bf16[2,4,96,384]{3,2,1,0:T(8,128)(2,1)S(1)} %pad_maximum_fusion.6.rest_0_), channel_id=1, source_target_pairs={{0,16},{4,20},{8,24},{12,28},{16,0},{20,4},{24,8},{28,12},{1,17},{... | collective-permute-start | bytes 1769480 | tf_op jit(solution)/shard_map/ppermute | solution.py:863
  66.1 26.5 %collective-permute-start.7 = (bf16[2,4,96,384]{3,2,1,0:T(8,128)(2,1)}, bf16[2,4,96,384]{3,2,1,0:T(8,128)(2,1)}, u32[]{:S(2)}, u32[]{:S(2)}) collective-permute-start(bf16[2,4,96,384]{3,2,1,0:T(8,128)(2,1)} %collective-permute-done.2.rest_2_), channel_id=1, source_target_pairs={{0,8},{4,12},{8,0},{12,4},{16,24},{20,28},{24,16},{28,20},{1,9},{5... | collective-permute-start | bytes 1769480 | tf_op jit(solution)/shard_map/ppermute | solution.py:863
  69.2 26.7 %collective-permute-start.9 = (bf16[2,4,96,384]{3,2,1,0:T(8,128)(2,1)}, bf16[2,4,96,384]{3,2,1,0:T(8,128)(2,1)S(1)}, u32[]{:S(2)}, u32[]{:S(2)}) collective-permute-start(bf16[2,4,96,384]{3,2,1,0:T(8,128)(2,1)} %collective-permute-done.3.rest_4_), channel_id=1, source_target_pairs={{0,4},{4,0},{8,12},{12,8},{16,20},{20,16},{24,28},{28,24},{1,5},{5... | collective-permute-start | bytes 1769480 | tf_op jit(solution)/shard_map/ppermute | solution.py:859
  95.9 29.1 %collective-permute-start.11 = (bf16[2,4,96,384]{3,2,1,0:T(8,128)(2,1)}, bf16[2,4,96,384]{3,2,1,0:T(8,128)(2,1)}, u32[]{:S(2)}, u32[]{:S(2)}) collective-permute-start(bf16[2,4,96,384]{3,2,1,0:T(8,128)(2,1)} %collective-permute-done.6.rest_2_), channel_id=1, source_target_pairs={{0,4},{4,0},{8,12},{12,8},{16,20},{20,16},{24,28},{28,24},{1,5},{5... | collective-permute-start | bytes 1769480 | tf_op jit(solution)/shard_map/ppermute | solution.py:859
  96.7 28.3 %collective-permute-start.13 = (bf16[2,4,96,384]{3,2,1,0:T(8,128)(2,1)}, bf16[2,4,96,384]{3,2,1,0:T(8,128)(2,1)}, u32[]{:S(2)}, u32[]{:S(2)}) collective-permute-start(bf16[2,4,96,384]{3,2,1,0:T(8,128)(2,1)} %collective-permute-done.6.rest_2_), channel_id=1, source_target_pairs={{0,8},{4,12},{8,0},{12,4},{16,24},{20,28},{24,16},{28,20},{1,9},{5... | collective-permute-start | bytes 1769480 | tf_op jit(solution)/shard_map/ppermute | solution.py:863
  98.6 26.4 %collective-permute-start.10 = (bf16[2,4,96,384]{3,2,1,0:T(8,128)(2,1)}, bf16[2,4,96,384]{3,2,1,0:T(8,128)(2,1)}, u32[]{:S(2)}, u32[]{:S(2)}) collective-permute-start(bf16[2,4,96,384]{3,2,1,0:T(8,128)(2,1)} %collective-permute-done.7.rest_6_), channel_id=1, source_target_pairs={{0,4},{4,0},{8,12},{12,8},{16,20},{20,16},{24,28},{28,24},{1,5},{5... | collective-permute-start | bytes 1769480 | tf_op jit(solution)/shard_map/ppermute | solution.py:859
  126.5 37.7 %collective-permute-start.16 = (bf16[2,4,96,384]{3,2,1,0:T(8,128)(2,1)}, bf16[2,4,96,384]{3,2,1,0:T(8,128)(2,1)S(1)}, u32[]{:S(2)}, u32[]{:S(2)}) collective-permute-start(bf16[2,4,96,384]{3,2,1,0:T(8,128)(2,1)} %collective-permute-done.12.rest_4_), channel_id=1, source_target_pairs={{0,4},{4,0},{8,12},{12,8},{16,20},{20,16},{24,28},{28,24},{1,5},{5... | collective-permute-start | bytes 1769480 | tf_op jit(solution)/shard_map/ppermute | solution.py:859
  127.3 36.9 %collective-permute-start.17 = (bf16[2,4,96,384]{3,2,1,0:T(8,128)(2,1)}, bf16[2,4,96,384]{3,2,1,0:T(8,128)(2,1)S(1)}, u32[]{:S(2)}, u32[]{:S(2)}) collective-permute-start(bf16[2,4,96,384]{3,2,1,0:T(8,128)(2,1)} %collective-permute-done.13.rest_6_), channel_id=1, source_target_pairs={{0,4},{4,0},{8,12},{12,8},{16,20},{20,16},{24,28},{28,24},{1,5},{5... | collective-permute-start | bytes 1769480 | tf_op jit(solution)/shard_map/ppermute | solution.py:859
  165.1 30.6 %collective-permute-start.18 = (bf16[8,192,192]{2,1,0:T(8,128)(2,1)}, bf16[8,192,192]{2,1,0:T(8,128)(2,1)S(1)}, u32[]{:S(2)}, u32[]{:S(2)}) collective-permute-start(bf16[8,192,192]{2,1,0:T(8,128)(2,1)} %get-tuple-element.333.o1), channel_id=1, source_target_pairs={{0,1},{1,0},{2,3},{3,2},{4,5},{5,4},{6,7},{7,6},{8,9},{9,8},{10,11... | collective-permute-start | bytes 1769480 | tf_op jit(solution)/shard_map/ppermute | solution.py:855
  306.3 28.5 %collective-permute-start.22 = (bf16[4,4,96,384]{3,2,1,0:T(8,128)(2,1)}, bf16[4,4,96,384]{3,2,1,0:T(8,128)(2,1)S(1)}, u32[]{:S(2)}, u32[]{:S(2)}) collective-permute-start(bf16[4,4,96,384]{3,2,1,0:T(8,128)(2,1)} %get-tuple-element.363), channel_id=1, source_target_pairs={{0,4},{4,0},{8,12},{12,8},{16,20},{20,16},{24,28},{28,24},{1,5},{5... | collective-permute-start | bytes 3538952 | tf_op jit(solution)/shard_map/ppermute | solution.py:859
  335.7 27.6 %collective-permute-start.25 = (bf16[4,4,96,384]{3,2,1,0:T(8,128)(2,1)}, bf16[4,4,96,384]{3,2,1,0:T(8,128)(2,1)}, u32[]{:S(2)}, u32[]{:S(2)}) collective-permute-start(bf16[4,4,96,384]{3,2,1,0:T(8,128)(2,1)} %get-tuple-element.379), channel_id=1, source_target_pairs={{0,4},{4,0},{8,12},{12,8},{16,20},{20,16},{24,28},{28,24},{1,5},{5... | collective-permute-start | bytes 3538952 | tf_op jit(solution)/shard_map/ppermute | solution.py:859
  364.9 27.3 %collective-permute-start.29 = (bf16[4,192,768]{2,1,0:T(8,128)(2,1)S(1)}, bf16[4,192,768]{2,1,0:T(8,128)(2,1)}, u32[]{:S(2)}, u32[]{:S(2)}) collective-permute-start(bf16[4,192,768]{2,1,0:T(8,128)(2,1)S(1)} %add_convert_fusion.1), channel_id=1, source_target_pairs={{0,2},{1,3},{2,0},{3,1},{4,6},{5,7},{6,4},{7,5},{8,10},{9,11},{10,... | collective-permute-start | bytes 3538952 | tf_op jit(solution)/shard_map/ppermute | solution.py:855
  370.7 27.4 %collective-permute-start.31 = (bf16[4,4,96,384]{3,2,1,0:T(8,128)(2,1)}, bf16[4,4,96,384]{3,2,1,0:T(8,128)(2,1)S(1)}, u32[]{:S(2)}, u32[]{:S(2)}) collective-permute-start(bf16[4,4,96,384]{3,2,1,0:T(8,128)(2,1)} %get-tuple-element.400), channel_id=1, source_target_pairs={{0,4},{4,0},{8,12},{12,8},{16,20},{20,16},{24,28},{28,24},{1,5},{5... | collective-permute-start | bytes 3538952 | tf_op jit(solution)/shard_map/ppermute | solution.py:859
  392.2 30.0 %collective-permute-start.33 = (bf16[4,4,96,384]{3,2,1,0:T(8,128)(2,1)}, bf16[4,4,96,384]{3,2,1,0:T(8,128)(2,1)}, u32[]{:S(2)}, u32[]{:S(2)}) collective-permute-start(bf16[4,4,96,384]{3,2,1,0:T(8,128)(2,1)} %get-tuple-element.402), channel_id=1, source_target_pairs={{0,4},{4,0},{8,12},{12,8},{16,20},{20,16},{24,28},{28,24},{1,5},{5... | collective-permute-start | bytes 3538952 | tf_op jit(solution)/shard_map/ppermute | solution.py:859
  405.2 50.9 %collective-permute-start.26 = (bf16[4,192,768]{2,1,0:T(8,128)(2,1)}, bf16[4,192,768]{2,1,0:T(8,128)(2,1)}, u32[]{:S(2)}, u32[]{:S(2)}) collective-permute-start(bf16[4,192,768]{2,1,0:T(8,128)(2,1)} %get-tuple-element.387), channel_id=1, source_target_pairs={{0,1},{1,0},{2,3},{3,2},{4,5},{5,4},{6,7},{7,6},{8,9},{9,8},{10,11... | collective-permute-start | bytes 3538952 | tf_op jit(solution)/shard_map/ppermute | solution.py:855
  433.0 40.6 %collective-permute-start.40 = (bf16[4,480,384]{2,1,0:T(8,128)(2,1)}, bf16[4,480,384]{2,1,0:T(8,128)(2,1)}, u32[]{:S(2)}, u32[]{:S(2)}) collective-permute-start(bf16[4,480,384]{2,1,0:T(8,128)(2,1)} %slice.329), channel_id=1, source_target_pairs={{0,4},{4,0},{8,12},{12,8},{16,20},{20,16},{24,28},{28,24},{1,5},{5... | collective-permute-start | bytes 4423688 | tf_op jit(solution)/shard_map/ppermute | solution.py:859
  446.4 27.3 %collective-permute-start.41 = (bf16[8,96,576]{2,1,0:T(8,128)(2,1)}, bf16[8,96,576]{2,1,0:T(8,128)(2,1)}, u32[]{:S(2)}, u32[]{:S(2)}) collective-permute-start(bf16[8,96,576]{2,1,0:T(8,128)(2,1)} %get-tuple-element.433), channel_id=1, source_target_pairs={{0,2},{1,3},{2,0},{3,1},{4,6},{5,7},{6,4},{7,5},{8,10},{9,11},{10,... | collective-permute-start | bytes 2654216 | tf_op jit(solution)/shard_map/ppermute | solution.py:855
  480.6 29.8 %collective-permute-start.46 = (bf16[2,480,384]{2,1,0:T(8,128)(2,1)}, bf16[2,480,384]{2,1,0:T(8,128)(2,1)S(1)}, u32[]{:S(2)}, u32[]{:S(2)}) collective-permute-start(bf16[2,480,384]{2,1,0:T(8,128)(2,1)} %add_convert_fusion.3), channel_id=1, source_target_pairs={{0,8},{4,12},{8,0},{12,4},{16,24},{20,28},{24,16},{28,20},{1,9},{5... | collective-permute-start | bytes 2211848 | tf_op jit(solution)/shard_map/ppermute | solution.py:863
  484.2 26.2 %collective-permute-start.45 = (bf16[4,96,576]{2,1,0:T(8,128)(2,1)}, bf16[4,96,576]{2,1,0:T(8,128)(2,1)}, u32[]{:S(2)}, u32[]{:S(2)}) collective-permute-start(bf16[4,96,576]{2,1,0:T(8,128)(2,1)} %slice.386), channel_id=1, source_target_pairs={{0,4},{4,0},{8,12},{12,8},{16,20},{20,16},{24,28},{28,24},{1,5},{5... | collective-permute-start | bytes 1327112 | tf_op jit(solution)/shard_map/ppermute | solution.py:859
  (92 other events, 919.6 us)
Sparse Core Ops, SparseCore 0:
  277.9 91.0 reduce-scatter.1

commit v2 on v1

--- a/solution.py
+++ b/solution.py
@@ -513,14 +513,19 @@
         gw_ref[...] = total
 
 
-def pair_back(meta, low, inv, raw, w, grads, *, few, blocks, group):
+def pair_weights(w, group):
+    cz = w.shape[0]
+    mean = jnp.mean(w.astype(f32), axis=0, keepdims=True)
+    w2 = jnp.concatenate([blocked(w, group), blocked(jnp.broadcast_to(-mean, w.shape).astype(bf16), group)], axis=0)
+    ones = blocked(jnp.full(w.shape, 1.0 / cz, bf16), group)
+    return w2, jnp.concatenate([ones, ones], axis=0)
+
+
+def pair_back(meta, low, inv, raw, weights, grads, *, few, blocks, group):
     ncx, rows, columns, cz = low.shape
     heads = few * blocks
     lines, spec, thin, _ = pair_specs(low, heads, group)
-    mean = jnp.mean(w.astype(f32), axis=0, keepdims=True)
-    w2 = jnp.concatenate([blocked(w, group), blocked(jnp.broadcast_to(-mean, w.shape).astype(bf16), group)], axis=0)
-    ones = blocked(jnp.full(w.shape, 1.0 / cz, bf16), group)
-    ones = jnp.concatenate([ones, ones], axis=0)
+    w2, ones = weights
     return pl.pallas_call(
         functools.partial(pair_back_kernel, few=few, blocks=blocks, group=group),
         grid_spec=pltpu.PrefetchScalarGridSpec(
@@ -1050,7 +1055,8 @@
 
         block_out, d_mid, d_xg, da0, da1, da2, da3, s_ac, s_scale2, s_tc, s_gain2, w_mid = middle_one(x_one, gates, atts)
         near_att = [swap(by_sample(v), 1) for v in (da1, da3)]
-        near_att, w_mid = fence(near_att, w_mid)
+        w_two = pair_weights(tie(w_pair, da1), group)
+        near_att, w_mid, w_two = fence(near_att, w_mid, w_two)
         mid = lax.psum_scatter(w_mid, "head", scatter_dimension=0, tiled=False)
 
         dq_0, dkv_0, *db_0 = back_one(kept[0], by_sample(da0), near_att[0])
@@ -1110,7 +1116,7 @@
         far_l = swap(low(keep_l[1], near_l[1]), 2)
         pair_grads = [jnp.stack([v[..., :rows] for v in sums[2 * k : 2 * k + 2]]) for k in halves]
         pair_grads += [far_rows[:2], far_rows[2:]]
-        grad_pair, grad_pair_weight = pair_back(pair_meta, pair_low, pair_inverse, pair_raw, w_pair, pair_grads, **sizes)
+        grad_pair, grad_pair_weight = pair_back(pair_meta, pair_low, pair_inverse, pair_raw, w_two, pair_grads, **sizes)
         far_l, got_h, z_m, grad_pair_weight = fence(far_l, got_h, z_m, grad_pair_weight)
         late = total_step(jnp.concatenate([grad_pair_weight.reshape(-1), others]), 0)
         keep_l, got_l = x_step(low(keep_l[0], near_l[0], far_l))
@@ -1144,6 +1150,7 @@
         late = total_step(total_step(late, 3), 4)
     else:
         w_heads, b_heads, w_q, w_kv = own_heads(w_query, w_key, w_value, b_query)
+        w_two = pair_weights(w_pair, group)
         biases = []
         for own in owns:
             gathered = lax.all_gather(own, "samp", axis=0)
@@ -1170,7 +1177,7 @@
             single_t, cond_t, d_mid, *weights_one, fast,
         )
         pair_grads = [v[..., :rows] for v in sums] + [swap(v[..., rows:], 1) for v in sums]
-        grad_pair, grad_pair_weight = pair_back(pair_meta, pair_low, pair_inverse, pair_raw, w_pair, pair_grads, **sizes)
+        grad_pair, grad_pair_weight = pair_back(pair_meta, pair_low, pair_inverse, pair_raw, w_two, pair_grads, **sizes)
 
         def total_of(stack):
             axis = stack.ndim - 1

time: 574 us -> 590 us (1.028)
  local copies, waits for them, and re-layouts: 29 us -> 36.9 us
    ppermute x22, waiting for transfers between devices: 68.5 us -> 83.5 us  [slot(): return lax.ppermute(value, 'samp', [(i, i ^ 2 * bit) for i in range(8)])]
    ppermute x15, waiting for transfers between devices: 31.4 us -> 22.4 us  [across(): return lax.ppermute(value, 'samp', [(i, i ^ 1) for i in range(8)])]
  transfers between devices with their start and end apart: 60 -> 60, of which waited for: 27 -> 26; matrix products, arithmetic and copies ran while one was open for 9% -> 11% of each run, Pallas kernels for 37% -> 36%
where the time goes in v2:
time: 590 us; the launch traced here: 580 us
  Pallas kernels  299 us (51%)
  waiting for transfers between devices  119 us (20%)
  starting transfers between devices  59.6 us (10%)
  other arithmetic  49.3 us (8%)
  local copies, waits for them, and re-layouts  36.9 us (6%)
  between operations  15.4 us (3%)
    ppermute x22, waiting for transfers between devices, slot(): return lax.ppermute(value, 'samp', [(i, i ^ 2 * bit) for i in range(8)])  83.5 us
    pallas_call x1, Pallas kernels, middle(): pl.pallas_call(functools.partial(middle_kernel, tiles=tiles, fast=fast),...  75 us
    pallas_call x2, Pallas kernels, attend(): pl.pallas_call(kern, grid_spec=pltpu.PrefetchScalarGridSpec(num_scalar_pr...  59.6 us
    pallas_call x2, Pallas kernels, attend_back(): pl.pallas_call(kern, grid_spec=pltpu.PrefetchScalarGridSpec(num_scalar_pr...  54.6 us
    pallas_call x2, Pallas kernels, heads_back(): pl.pallas_call(functools.partial(heads_back_kernel, parts=parts, rows=row...  34.9 us
    ppermute x22, starting transfers between devices, slot(): return lax.ppermute(value, 'samp', [(i, i ^ 2 * bit) for i in range(8)])  30.7 us
    convert_element_type x23, other arithmetic, low(): return add(*terms).astype(bf16)  26.2 us
    ppermute x15, waiting for transfers between devices, across(): return lax.ppermute(value, 'samp', [(i, i ^ 1) for i in range(8)])  22.4 us
  transfers between devices with their start and end apart: 60, of which 26 were waited for; matrix products, arithmetic and copies ran while one was open for 11% of the time, Pallas kernels for 36%

profile of v2, /device:TPU:0, one launch (start us, length us, event | category | flops | bytes accessed | tf_op | source)
XLA Modules:
  0.0 579.9 jit_solution(16338365119731869670)
XLA Ops:
  9.5 15.8 %pair_bias.1 = (bf16[2,192,96,128]{3,2,1,0:T(8,128)(2,1)}, f32[2,24,96,128]{3,2,1,0:T(8,128)}, f32[2,24,96,128]{3,2,1,0:T(8,128)}, bf16[2,4,96,192]{3,2,1,0:T(8,...) custom-call(s32[2]{0:T(128)} %pad_add_fusion.1.meta, ...), custom_call_target="tpu_custom_call" | custom-call | flops 1048576 | bytes 1048576 | tf_op jit(solution)/shard_map/pair_bias/pallas_call | solution.py:445
  39.4 8.0 %adapt.1.x_ref = bf16[1536,768]{1,0:T(8,128)(2,1)} custom-call(bf16[1536,768]{1,0:T(8,128)(2,1)} %bitcast.126, bf16[1536,384]{1,0:T(8,128)(2,1)} %bitcast.129, bf16[1,384]{1,0:T(2,128)(2,1)} %reshape.280.gain, bf16[384,768]{1,0:T(8,128)(2,1)} %w_scale.7, bf16[1,768]{1,0:T(2,128)(2,1)} %reshape.281.b_scale, bf16[384,768]{1,0:T(8,128)(2,1)} %w_shift.7), custom_call_target="tpu_custom_call" | custom-call | flops 1048576 | bytes 1048576 | tf_op jit(solution)/shard_map/adapt/pallas_call | solution.py:566
  47.5 14.2 %collective-permute-done.3.rest_4_ = bf16[2,4,96,384]{3,2,1,0:T(8,128)(2,1)S(1)} collective-permute-done((bf16[2,4,96,384]{3,2,1,0:T(8,128)(2,1)S(1)}, bf16[2,4,96,384]{3,2,1,0:T(8,128)(2,1)S(1)}, u32[]{:S(2)}, u32[]{:S(2)}) %collective-permute-start.3) | collective-permute-done | bytes 589856 | tf_op jit(solution)/shard_map/ppermute | solution.py:868
  75.1 16.2 %collective-permute-done.6.rest_2_ = bf16[2,4,96,384]{3,2,1,0:T(8,128)(2,1)} collective-permute-done((bf16[2,4,96,384]{3,2,1,0:T(8,128)(2,1)}, bf16[2,4,96,384]{3,2,1,0:T(8,128)(2,1)}, u32[]{:S(2)}, u32[]{:S(2)}) %collective-permute-start.6) | collective-permute-done | bytes 589856 | tf_op jit(solution)/shard_map/ppermute | solution.py:868
  103.3 16.3 %before.1 = (f32[1536,768]{1,0:T(8,128)}, f32[1536,768]{1,0:T(8,128)}, f32[1536,768]{1,0:T(8,128)}, f32[1536,768]{1,0:T(8,128)}, bf16[1536,768]{1,0:T(8,128)(2,1)}, /*index=5*/bf16[1536,1536]{1,0:T(8,128)(2,1)}) custom-call(bf16[1536,768]{1,0:T(8,128)(2,1)} %adapt.1.x_ref, bf16[1536,384]{1,0:T(8,128)(2,1)} %bitcast.130, bf16[1536,768]{1,0:T(8,128)(2,1)} %bitcast.133, ...), custom_call_target="tpu_custom_call" | custom-call | flops 1048576 | bytes 1048576 | tf_op jit(solution)/shard_map/before/pallas_call | solution.py:609
  133.1 30.0 %attend.2 = (bf16[8,192,192]{2,1,0:T(8,128)(2,1)}, bf16[8,192,192]{2,1,0:T(8,128)(2,1)}, bf16[8,4,768,384]{3,2,1,0:T(8,128)(2,1)}, bf16[8,192,384]{2,1,0:T(8,128...) custom-call(s32[22]{0:T(128)} %concatenate.39.meta, ...), custom_call_target="tpu_custom_call" | custom-call | flops 1048576 | bytes 1048576 | tf_op jit(solution)/shard_map/attend/pallas_call | solution.py:135
  164.2 29.6 %attend.3 = (bf16[8,192,192]{2,1,0:T(8,128)(2,1)}, bf16[8,192,192]{2,1,0:T(8,128)(2,1)}, bf16[8,4,768,384]{3,2,1,0:T(8,128)(2,1)}, bf16[8,192,384]{2,1,0:T(8,128...) custom-call(s32[22]{0:T(128)} %concatenate.39.meta, ...), custom_call_target="tpu_custom_call" | custom-call | flops 1048576 | bytes 1048576 | tf_op jit(solution)/shard_map/attend/pallas_call | solution.py:135
  197.3 75.0 %middle.1 = (bf16[1536,768]{1,0:T(8,128)(2,1)}, f32[1536,768]{1,0:T(8,128)}, bf16[1536,768]{1,0:T(8,128)(2,1)}, bf16[1536,192]{1,0:T(8,128)(2,1)}, bf16[1536,192...) custom-call(s32[22]{0:T(128)} %concatenate.39.meta, ...), custom_call_target="tpu_custom_call" | custom-call | flops 1048576 | bytes 1048576 | tf_op jit(solution)/shard_map/middle/pallas_call | solution.py:760
  277.0 28.0 %attend_back.2 = (bf16[8,192,384]{2,1,0:T(8,128)(2,1)}, bf16[8,384,768]{2,1,0:T(8,128)(2,1)}, bf16[4,4,96,384]{3,2,1,0:T(8,128)(2,1)}, bf16[4,4,96,384]{3,2,1,0:...) custom-call(s32[22]{0:T(128)} %concatenate.39.meta, ...), custom_call_target="tpu_custom_call" | custom-call | flops 1048576 | bytes 1048576 | tf_op jit(solution)/shard_map/attend_back/pallas_call | solution.py:256
  305.3 26.6 %attend_back.3 = (bf16[8,192,384]{2,1,0:T(8,128)(2,1)}, bf16[8,384,768]{2,1,0:T(8,128)(2,1)}, bf16[4,4,96,384]{3,2,1,0:T(8,128)(2,1)}, bf16[4,4,96,384]{3,2,1,0:...) custom-call(s32[22]{0:T(128)} %concatenate.39.meta, ...), custom_call_target="tpu_custom_call" | custom-call | flops 1048576 | bytes 1048576 | tf_op jit(solution)/shard_map/attend_back/pallas_call | solution.py:256
  335.7 15.7 %heads_back.2 = (bf16[4,192,768]{2,1,0:T(8,128)(2,1)}, bf16[4,192,768]{2,1,0:T(8,128)(2,1)}, bf16[4,192,768]{2,1,0:T(8,128)(2,1)}, bf16[4,192,768]{2,1,0:T(8,128...) custom-call(s32[22]{0:T(128)} %concatenate.39.meta, bf16[8,192,768]{2,1,0:T(8,128)(2,1)} %bitcast.124, ...), custom_call_target="tpu_custom_call" | custom-call | flops 1048576 | bytes 1048576 | tf_op jit(solution)/shard_map/heads_back/pallas_call | solution.py:350
  351.5 10.3 %collective-permute-done.25 = bf16[4,4,96,384]{3,2,1,0:T(8,128)(2,1)S(1)} collective-permute-done((bf16[4,4,96,384]{3,2,1,0:T(8,128)(2,1)}, bf16[4,4,96,384]{3,2,1,0:T(8,128)(2,1)S(1)}, u32[]{:S(2)}, u32[]{:S(2)}) %collective-permute-start.25) | collective-permute-done | bytes 1179680 | tf_op jit(solution)/shard_map/ppermute | solution.py:864
  371.7 19.2 %heads_back.3 = (bf16[4,192,768]{2,1,0:T(8,128)(2,1)}, bf16[4,192,768]{2,1,0:T(8,128)(2,1)}, bf16[4,192,768]{2,1,0:T(8,128)(2,1)}, bf16[4,192,768]{2,1,0:T(8,128...) custom-call(s32[22]{0:T(128)} %concatenate.39.meta, ...), custom_call_target="tpu_custom_call" | custom-call | flops 1048576 | bytes 1048576 | tf_op jit(solution)/shard_map/heads_back/pallas_call | solution.py:350
  405.5 15.2 %collective-permute-done.35 = bf16[4,96,384]{2,1,0:T(8,128)(2,1)S(1)} collective-permute-done((bf16[4,96,384]{2,1,0:T(8,128)(2,1)S(1)}, bf16[4,96,384]{2,1,0:T(8,128)(2,1)S(1)}, u32[]{:S(2)}, u32[]{:S(2)}) %collective-permute-start.35) | collective-permute-done | bytes 294944 | tf_op jit(solution)/shard_map/ppermute | solution.py:868
  423.3 3.3 collective-permute-done.32
  435.7 11.3 %collective-permute-done.37 = bf16[4,96,384]{2,1,0:T(8,128)(2,1)S(1)} collective-permute-done((bf16[4,96,384]{2,1,0:T(8,128)(2,1)S(1)}, bf16[4,96,384]{2,1,0:T(8,128)(2,1)S(1)}, u32[]{:S(2)}, u32[]{:S(2)}) %collective-permute-start.37) | collective-permute-done | bytes 294944 | tf_op jit(solution)/shard_map/ppermute | solution.py:868
  461.6 17.5 %last.1 = (f32[1536,768]{1,0:T(8,128)}, f32[1,768]{1,0:T(1,128)}, f32[1,384]{1,0:T(1,128)}, bf16[2,8,48,384]{3,2,1,0:T(8,128)(2,1)}, bf16[2,8,48,384]{3,2,1,0:T(8,128)(2,1)}) custom-call(s32[22]{0:T(128)} %concatenate.39.meta, bf16[768,768]{1,0:T(8,128)(2,1)} %bitcast.141, bf16[768,768]{1,0:T(8,128)(2,1)} %bitcast.142, bf16[768,768]{1,0:T(8,128)(2,1)} %bitcast.42.d2, ...), custom_call_target="tpu_custom_call" | custom-call | flops 1048576 | bytes 1048576 | tf_op jit(solution)/shard_map/last/pallas_call | solution.py:840
  479.9 4.9 collective-permute-done.40
  495.7 3.1 collective-permute-start.46
  504.9 17.5 %pair_back.1 = (f32[2,192,96,128]{3,2,1,0:T(8,128)}, f32[16,128]{1,0:T(8,128)}) custom-call(s32[2]{0:T(128)} %pad_add_fusion.1.meta, bf16[2,192,96,128]{3,2,1,0:T(8,128)(2,1)} %get-tuple-element.429.low_ref, f32[2,24,96,128]{3,2,1,0:T(8,128)} %get-tuple-element.430.inv_ref, f32[2,24,96,128]{3,2,1,0:T(8,128)} %get-tuple-element.431.raw_ref, ...), custom_call_target="tpu_custom_call" | custom-call | flops 1048576 | bytes 1048576 | tf_op jit(solution)/shard_map/pair_back/pallas_call | solution.py:529
  534.2 6.6 %collective-permute-done.50 = bf16[2,48,384]{2,1,0:T(8,128)(2,1)S(1)} collective-permute-done((bf16[2,48,384]{2,1,0:T(8,128)(2,1)S(1)}, bf16[2,48,384]{2,1,0:T(8,128)(2,1)S(1)}, u32[]{:S(2)}, u32[]{:S(2)}) %collective-permute-start.50) | collective-permute-done | bytes 73760 | tf_op jit(solution)/shard_map/ppermute | solution.py:868
  540.8 5.5 collective-permute-done.52
  556.7 4.2 collective-permute-done.55
  567.1 3.7 collective-permute-done.57
  (338 shorter events, 166.6 us)
Async XLA Ops:
  7.2 419.4 %reduce-scatter.2.cloned.1.call-start = ((), (), s32[]{:S(2)}) async-start(), calls=%async_computation.1 | async-start | bytes 14745600 | tf_op jit(solution)/shard_map/reduce_scatter | solution.py:1060
  31.2 33.0 %collective-permute-start.4 = (bf16[2,2,4,96,384]{4,3,2,1,0:T(8,128)(2,1)S(1)}, bf16[2,2,4,96,384]{4,3,2,1,0:T(8,128)(2,1)S(1)}, u32[]{:S(2)}, u32[]{:S(2)}) collective-permute-start(bf16[2,2,4,96,384]{4,3,2,1,0:T(8,128)(2,1)S(1)} %pad_maximum_fusion), channel_id=1, source_target_pairs={{0,4},{4,0},{8,12},{12,8},{16,20},{20,16},{24,28},{28,24},{1,5},{5... | collective-permute-start | bytes 3538952 | tf_op jit(solution)/shard_map/ppermute | solution.py:864
  34.1 27.6 %collective-permute-start.3 = (bf16[2,4,96,384]{3,2,1,0:T(8,128)(2,1)S(1)}, bf16[2,4,96,384]{3,2,1,0:T(8,128)(2,1)S(1)}, u32[]{:S(2)}, u32[]{:S(2)}) collective-permute-start(bf16[2,4,96,384]{3,2,1,0:T(8,128)(2,1)S(1)} %pad_maximum_fusion.5.rest_0_), channel_id=1, source_target_pairs={{0,8},{4,12},{8,0},{12,4},{16,24},{20,28},{24,16},{28,20},{1,9},{5... | collective-permute-start | bytes 1769480 | tf_op jit(solution)/shard_map/ppermute | solution.py:868
  35.7 28.5 %collective-permute-start.2 = (bf16[2,4,96,384]{3,2,1,0:T(8,128)(2,1)S(1)}, bf16[2,4,96,384]{3,2,1,0:T(8,128)(2,1)}, u32[]{:S(2)}, u32[]{:S(2)}) collective-permute-start(bf16[2,4,96,384]{3,2,1,0:T(8,128)(2,1)S(1)} %pad_maximum_fusion.5.rest_0_), channel_id=1, source_target_pairs={{0,16},{4,20},{8,24},{12,28},{16,0},{20,4},{24,8},{28,12},{1,17},{... | collective-permute-start | bytes 1769480 | tf_op jit(solution)/shard_map/ppermute | solution.py:868
  64.2 59.6 %collective-permute-start.5 = (bf16[1536,768]{1,0:T(8,128)(2,1)}, bf16[1536,768]{1,0:T(8,128)(2,1)}, u32[]{:S(2)}, u32[]{:S(2)}) collective-permute-start(bf16[1536,768]{1,0:T(8,128)(2,1)} %adapt.1.x_ref), channel_id=1, source_target_pairs={{0,2},{1,3},{2,0},{3,1},{4,6},{5,7},{6,4},{7,5},{8,10},{9,11},{10,... | collective-permute-start | bytes 7077896 | tf_op jit(solution)/shard_map/ppermute | solution.py:860
  66.6 25.7 %collective-permute-start.8 = (bf16[2,4,96,384]{3,2,1,0:T(8,128)(2,1)}, bf16[2,4,96,384]{3,2,1,0:T(8,128)(2,1)S(1)}, u32[]{:S(2)}, u32[]{:S(2)}) collective-permute-start(bf16[2,4,96,384]{3,2,1,0:T(8,128)(2,1)} %collective-permute-done.2.rest_2_), channel_id=1, source_target_pairs={{0,4},{4,0},{8,12},{12,8},{16,20},{20,16},{24,28},{28,24},{1,5},{5... | collective-permute-start | bytes 1769480 | tf_op jit(solution)/shard_map/ppermute | solution.py:864
  92.3 31.4 %collective-permute-start.13 = (bf16[2,4,96,384]{3,2,1,0:T(8,128)(2,1)}, bf16[2,4,96,384]{3,2,1,0:T(8,128)(2,1)}, u32[]{:S(2)}, u32[]{:S(2)}) collective-permute-start(bf16[2,4,96,384]{3,2,1,0:T(8,128)(2,1)} %collective-permute-done.6.rest_2_), channel_id=1, source_target_pairs={{0,8},{4,12},{8,0},{12,4},{16,24},{20,28},{24,16},{28,20},{1,9},{5... | collective-permute-start | bytes 1769480 | tf_op jit(solution)/shard_map/ppermute | solution.py:868
  93.0 30.7 %collective-permute-start.11 = (bf16[2,4,96,384]{3,2,1,0:T(8,128)(2,1)}, bf16[2,4,96,384]{3,2,1,0:T(8,128)(2,1)}, u32[]{:S(2)}, u32[]{:S(2)}) collective-permute-start(bf16[2,4,96,384]{3,2,1,0:T(8,128)(2,1)} %collective-permute-done.6.rest_2_), channel_id=1, source_target_pairs={{0,4},{4,0},{8,12},{12,8},{16,20},{20,16},{24,28},{28,24},{1,5},{5... | collective-permute-start | bytes 1769480 | tf_op jit(solution)/shard_map/ppermute | solution.py:864
  94.5 29.2 %collective-permute-start.10 = (bf16[2,4,96,384]{3,2,1,0:T(8,128)(2,1)}, bf16[2,4,96,384]{3,2,1,0:T(8,128)(2,1)}, u32[]{:S(2)}, u32[]{:S(2)}) collective-permute-start(bf16[2,4,96,384]{3,2,1,0:T(8,128)(2,1)} %collective-permute-done.7.rest_6_), channel_id=1, source_target_pairs={{0,4},{4,0},{8,12},{12,8},{16,20},{20,16},{24,28},{28,24},{1,5},{5... | collective-permute-start | bytes 1769480 | tf_op jit(solution)/shard_map/ppermute | solution.py:864
  95.1 28.7 %collective-permute-start.12 = (bf16[2,4,96,384]{3,2,1,0:T(8,128)(2,1)}, bf16[2,4,96,384]{3,2,1,0:T(8,128)(2,1)}, u32[]{:S(2)}, u32[]{:S(2)}) collective-permute-start(bf16[2,4,96,384]{3,2,1,0:T(8,128)(2,1)} %pad_maximum_fusion.6.rest_0_), channel_id=1, source_target_pairs={{0,8},{4,12},{8,0},{12,4},{16,24},{20,28},{24,16},{28,20},{1,9},{5... | collective-permute-start | bytes 1769480 | tf_op jit(solution)/shard_map/ppermute | solution.py:868
  125.2 37.9 %collective-permute-start.16 = (bf16[2,4,96,384]{3,2,1,0:T(8,128)(2,1)}, bf16[2,4,96,384]{3,2,1,0:T(8,128)(2,1)S(1)}, u32[]{:S(2)}, u32[]{:S(2)}) collective-permute-start(bf16[2,4,96,384]{3,2,1,0:T(8,128)(2,1)} %collective-permute-done.12.rest_4_), channel_id=1, source_target_pairs={{0,4},{4,0},{8,12},{12,8},{16,20},{20,16},{24,28},{28,24},{1,5},{5... | collective-permute-start | bytes 1769480 | tf_op jit(solution)/shard_map/ppermute | solution.py:864
  125.9 37.2 %collective-permute-start.17 = (bf16[2,4,96,384]{3,2,1,0:T(8,128)(2,1)}, bf16[2,4,96,384]{3,2,1,0:T(8,128)(2,1)S(1)}, u32[]{:S(2)}, u32[]{:S(2)}) collective-permute-start(bf16[2,4,96,384]{3,2,1,0:T(8,128)(2,1)} %collective-permute-done.13.rest_6_), channel_id=1, source_target_pairs={{0,4},{4,0},{8,12},{12,8},{16,20},{20,16},{24,28},{28,24},{1,5},{5... | collective-permute-start | bytes 1769480 | tf_op jit(solution)/shard_map/ppermute | solution.py:864
  163.1 30.7 %collective-permute-start.18 = (bf16[8,192,192]{2,1,0:T(8,128)(2,1)}, bf16[8,192,192]{2,1,0:T(8,128)(2,1)S(1)}, u32[]{:S(2)}, u32[]{:S(2)}) collective-permute-start(bf16[8,192,192]{2,1,0:T(8,128)(2,1)} %get-tuple-element.336.o1), channel_id=1, source_target_pairs={{0,1},{1,0},{2,3},{3,2},{4,5},{5,4},{6,7},{7,6},{8,9},{9,8},{10,11... | collective-permute-start | bytes 1769480 | tf_op jit(solution)/shard_map/ppermute | solution.py:860
  305.0 28.4 %collective-permute-start.22 = (bf16[4,4,96,384]{3,2,1,0:T(8,128)(2,1)}, bf16[4,4,96,384]{3,2,1,0:T(8,128)(2,1)S(1)}, u32[]{:S(2)}, u32[]{:S(2)}) collective-permute-start(bf16[4,4,96,384]{3,2,1,0:T(8,128)(2,1)} %get-tuple-element.367), channel_id=1, source_target_pairs={{0,4},{4,0},{8,12},{12,8},{16,20},{20,16},{24,28},{28,24},{1,5},{5... | collective-permute-start | bytes 3538952 | tf_op jit(solution)/shard_map/ppermute | solution.py:864
  334.1 27.6 %collective-permute-start.25 = (bf16[4,4,96,384]{3,2,1,0:T(8,128)(2,1)}, bf16[4,4,96,384]{3,2,1,0:T(8,128)(2,1)S(1)}, u32[]{:S(2)}, u32[]{:S(2)}) collective-permute-start(bf16[4,4,96,384]{3,2,1,0:T(8,128)(2,1)} %get-tuple-element.383), channel_id=1, source_target_pairs={{0,4},{4,0},{8,12},{12,8},{16,20},{20,16},{24,28},{28,24},{1,5},{5... | collective-permute-start | bytes 3538952 | tf_op jit(solution)/shard_map/ppermute | solution.py:864
  364.5 29.3 %collective-permute-start.29 = (bf16[4,192,768]{2,1,0:T(8,128)(2,1)S(1)}, bf16[4,192,768]{2,1,0:T(8,128)(2,1)}, u32[]{:S(2)}, u32[]{:S(2)}) collective-permute-start(bf16[4,192,768]{2,1,0:T(8,128)(2,1)S(1)} %add_convert_fusion.1), channel_id=1, source_target_pairs={{0,2},{1,3},{2,0},{3,1},{4,6},{5,7},{6,4},{7,5},{8,10},{9,11},{10,... | collective-permute-start | bytes 3538952 | tf_op jit(solution)/shard_map/ppermute | solution.py:860
  365.1 25.9 %collective-permute-start.28 = (bf16[2,4,96,384]{3,2,1,0:T(8,128)(2,1)S(1)}, bf16[2,4,96,384]{3,2,1,0:T(8,128)(2,1)}, u32[]{:S(2)}, u32[]{:S(2)}) collective-permute-start(bf16[2,4,96,384]{3,2,1,0:T(8,128)(2,1)S(1)} %add_convert_fusion.6), channel_id=1, source_target_pairs={{0,8},{4,12},{8,0},{12,4},{16,24},{20,28},{24,16},{28,20},{1,9},{5... | collective-permute-start | bytes 1769480 | tf_op jit(solution)/shard_map/ppermute | solution.py:868
  370.5 26.1 %collective-permute-start.31 = (bf16[4,4,96,384]{3,2,1,0:T(8,128)(2,1)}, bf16[4,4,96,384]{3,2,1,0:T(8,128)(2,1)S(1)}, u32[]{:S(2)}, u32[]{:S(2)}) collective-permute-start(bf16[4,4,96,384]{3,2,1,0:T(8,128)(2,1)} %get-tuple-element.404), channel_id=1, source_target_pairs={{0,4},{4,0},{8,12},{12,8},{16,20},{20,16},{24,28},{28,24},{1,5},{5... | collective-permute-start | bytes 3538952 | tf_op jit(solution)/shard_map/ppermute | solution.py:864
  393.8 28.7 %collective-permute-start.33 = (bf16[4,4,96,384]{3,2,1,0:T(8,128)(2,1)}, bf16[4,4,96,384]{3,2,1,0:T(8,128)(2,1)}, u32[]{:S(2)}, u32[]{:S(2)}) collective-permute-start(bf16[4,4,96,384]{3,2,1,0:T(8,128)(2,1)} %get-tuple-element.406), channel_id=1, source_target_pairs={{0,4},{4,0},{8,12},{12,8},{16,20},{20,16},{24,28},{28,24},{1,5},{5... | collective-permute-start | bytes 3538952 | tf_op jit(solution)/shard_map/ppermute | solution.py:864
  399.1 27.4 %collective-permute-start.32 = (bf16[4,192,768]{2,1,0:T(8,128)(2,1)S(1)}, bf16[4,192,768]{2,1,0:T(8,128)(2,1)}, u32[]{:S(2)}, u32[]{:S(2)}) collective-permute-start(bf16[4,192,768]{2,1,0:T(8,128)(2,1)S(1)} %add_convert_fusion), channel_id=1, source_target_pairs={{0,2},{1,3},{2,0},{3,1},{4,6},{5,7},{6,4},{7,5},{8,10},{9,11},{10,... | collective-permute-start | bytes 3538952 | tf_op jit(solution)/shard_map/ppermute | solution.py:860
  405.5 54.5 %collective-permute-start.26 = (bf16[4,192,768]{2,1,0:T(8,128)(2,1)}, bf16[4,192,768]{2,1,0:T(8,128)(2,1)}, u32[]{:S(2)}, u32[]{:S(2)}) collective-permute-start(bf16[4,192,768]{2,1,0:T(8,128)(2,1)} %get-tuple-element.391), channel_id=1, source_target_pairs={{0,1},{1,0},{2,3},{3,2},{4,5},{5,4},{6,7},{7,6},{8,9},{9,8},{10,11... | collective-permute-start | bytes 3538952 | tf_op jit(solution)/shard_map/ppermute | solution.py:860
  449.8 35.0 %collective-permute-start.40 = (bf16[4,480,384]{2,1,0:T(8,128)(2,1)}, bf16[4,480,384]{2,1,0:T(8,128)(2,1)S(1)}, u32[]{:S(2)}, u32[]{:S(2)}) collective-permute-start(bf16[4,480,384]{2,1,0:T(8,128)(2,1)} %slice.329), channel_id=1, source_target_pairs={{0,4},{4,0},{8,12},{12,8},{16,20},{20,16},{24,28},{28,24},{1,5},{5... | collective-permute-start | bytes 4423688 | tf_op jit(solution)/shard_map/ppermute | solution.py:864
  491.8 30.6 %collective-permute-start.45 = (bf16[4,96,576]{2,1,0:T(8,128)(2,1)}, bf16[4,96,576]{2,1,0:T(8,128)(2,1)}, u32[]{:S(2)}, u32[]{:S(2)}) collective-permute-start(bf16[4,96,576]{2,1,0:T(8,128)(2,1)} %slice.386), channel_id=1, source_target_pairs={{0,4},{4,0},{8,12},{12,8},{16,20},{20,16},{24,28},{28,24},{1,5},{5... | collective-permute-start | bytes 1327112 | tf_op jit(solution)/shard_map/ppermute | solution.py:864
  495.7 26.7 %collective-permute-start.46 = (bf16[2,480,384]{2,1,0:T(8,128)(2,1)}, bf16[2,480,384]{2,1,0:T(8,128)(2,1)}, u32[]{:S(2)}, u32[]{:S(2)}) collective-permute-start(bf16[2,480,384]{2,1,0:T(8,128)(2,1)} %add_convert_fusion.3), channel_id=1, source_target_pairs={{0,8},{4,12},{8,0},{12,4},{16,24},{20,28},{24,16},{28,20},{1,9},{5... | collective-permute-start | bytes 2211848 | tf_op jit(solution)/shard_map/ppermute | solution.py:868
  (98 other events, 1310.2 us)
Sparse Core Ops, SparseCore 0:
  276.2 95.6 reduce-scatter.1
